TPU v7x, 256 devices: a whole 4x4x8 slice. The times are simulated.
256 devices in a mesh: inst: 8 (over x_hi, y), slab: 32 (over z, x_lo, core).
Axes of the slice: x: 4 (x_hi: 2, x_lo: 2; x = x_hi * 2 + x_lo), y: 4, z: 8, core: 2. Of those that a mesh axis runs over, the one named last changes fastest.
Arguments:
- volume_frac: float32 [8, 256, 64, 512], P('inst', 'slab'), may hold values from 0 to 1
- velocity_u: float32 [8, 256, 64, 512], P('inst', 'slab'), may hold values from -6 to 6
- velocity_v: float32 [8, 256, 64, 512], P('inst', 'slab'), may hold values from -6 to 6
- velocity_w: float32 [8, 256, 64, 512], P('inst', 'slab'), may hold values from -6 to 6
- wetted: int32 [8, 256, 64, 512], P('inst', 'slab'), may hold values 0 or 1
- section_map: int32 [256, 64, 512], P('slab'), may hold values from 0 to 63, as said below
Outputs:
- residual: float32 [8, 256, 64, 512], P('inst', 'slab')
- section_loads: float32 [8, 2, 64], P('inst', None, 'slab')
Inputs may be any that keep to these rules, and one draw needn't show every extreme that they name: `section_map`: a cell in longitudinal column x maps to a section within one of x * 64 // 512.
All inputs are finite; a program needn't handle non-finite values. No bound on the sum of `wetted` on one device may be relied on, other than what follows from the above.
Results may differ from a plain program's by a relative error of at most 0.00022.
Values sent between devices are 32-bit elements; how exact they have to be, the bound alone decides.
A program may use at most 64 MiB of HBM per device.

v0:
```python
import jax
import jax.numpy as jnp
from jax import lax
from jax.sharding import PartitionSpec as P

CV = 8
NY = 64
NX = 512
SEC_DEV = 2


SIGMA = 1.0
GRAVITY = 4.0


def extended(block, sides, width):
    for axis, dim in sides:
        count = lax.axis_size(axis)
        forward = [(i, i + 1) for i in range(count - 1)]
        backward = [(target, source) for source, target in forward]
        low = lax.ppermute(
            lax.slice_in_dim(block, block.shape[dim] - width, None, axis=dim), axis, forward
        )
        high = lax.ppermute(lax.slice_in_dim(block, 0, width, axis=dim), axis, backward)
        block = jnp.concatenate([low, block, high], axis=dim)
    return block


def coef_table(count):
    steps = jnp.arange(count, dtype=jnp.int32)
    angle = jnp.pi / count * steps.astype(jnp.float32)
    parity = (1 - 2 * (steps % 2)).astype(jnp.float32)
    sine = jnp.where(steps == 0, jnp.float32(1.0), jnp.sin(angle))
    spectral = jnp.where(steps == 0, jnp.float32(0.0), 0.5 * parity * jnp.cos(angle) / sine)
    return spectral + SIGMA / count * parity


def upwind(field, speed, axis):
    length = field.shape[axis] - 2
    lower_f = lax.slice_in_dim(field, 0, length + 1, axis=axis)
    upper_f = lax.slice_in_dim(field, 1, length + 2, axis=axis)
    face_speed = 0.5 * (
        lax.slice_in_dim(speed, 0, length + 1, axis=axis)
        + lax.slice_in_dim(speed, 1, length + 2, axis=axis)
    )
    flux = jnp.maximum(face_speed, 0.0) * lower_f + jnp.minimum(face_speed, 0.0) * upper_f
    return lax.slice_in_dim(flux, 1, length + 1, axis=axis) - lax.slice_in_dim(
        flux, 0, length, axis=axis
    )


def pad_axis(field, axis):
    widths = [(0, 0), (0, 0), (0, 0)]
    widths[axis] = (1, 1)
    return jnp.pad(field, widths)


def on_device(volume_frac, velocity_u, velocity_v, velocity_w, wetted, section_map):
    n_inst = lax.axis_size("inst")
    n_slab = lax.axis_size("slab")
    instance = lax.axis_index("inst")
    slab_pos = lax.axis_index("slab")
    table = coef_table(n_inst)
    alpha = volume_frac[0]
    speed_u = velocity_u[0]
    speed_v = velocity_v[0]
    speed_w = velocity_w[0]
    layers, rows_y, cols_x = alpha.shape
    piece = lax.all_gather(volume_frac, "inst", axis=0, tiled=True)
    count = piece.shape[0]
    lags = (instance - jnp.arange(count, dtype=jnp.int32)) % n_inst
    picks = (lags[:, None] == jnp.arange(n_inst, dtype=jnp.int32)[None, :]).astype(jnp.float32)
    weights = jnp.sum(table[None, :] * picks, axis=1)
    derivative = jnp.sum(weights[:, None, None, None] * piece, axis=0)
    stacked = jnp.stack([alpha, speed_w])
    padded = extended(stacked, (("slab", 1),), 1)
    divergence = upwind(padded[0], padded[1], 0)
    divergence = divergence + upwind(pad_axis(alpha, 1), pad_axis(speed_v, 1), 1)
    divergence = divergence + upwind(pad_axis(alpha, 2), pad_axis(speed_u, 2), 2)
    residual = (derivative + divergence)[None]
    total_v = layers * n_slab
    global_v = slab_pos * layers + jnp.arange(layers, dtype=jnp.int32)
    depth = (global_v.astype(jnp.float32) + 0.5) / jnp.float32(total_v)
    lever = (jnp.arange(rows_y, dtype=jnp.int32).astype(jnp.float32) + 0.5) / jnp.float32(rows_y)
    pressure = GRAVITY * depth[:, None, None] + 0.5 * (
        speed_u * speed_u + speed_v * speed_v + speed_w * speed_w
    )
    load = wetted[0].astype(jnp.float32) * alpha * pressure
    both_loads = jnp.stack([load, load * lever[None, :, None]])
    nsec = SEC_DEV * n_slab
    base = jnp.arange(cols_x, dtype=jnp.int32) * nsec // cols_x
    sections = jnp.arange(nsec, dtype=jnp.int32)
    term = jnp.zeros((2, nsec), jnp.float32)
    for offset in (-1, 0, 1):
        target = base + offset
        match = section_map == target[None, None, :]
        columns = jnp.sum(jnp.where(match[None], both_loads, 0.0), axis=(1, 2))
        selector = (target[:, None] == sections[None, :]).astype(jnp.float32)
        term = term + jnp.dot(columns, selector, precision=lax.Precision.HIGHEST)
    term = term * jnp.float32(SEC_DEV / (CV * NY * NX))
    owned = lax.psum_scatter(term, "slab", scatter_dimension=1, tiled=True)
    return (residual, owned[None])


def solution(mesh):
    placed = (
        P("inst", "slab", None, None),
        P("inst", "slab", None, None),
        P("inst", "slab", None, None),
        P("inst", "slab", None, None),
        P("inst", "slab", None, None),
        P("slab", None, None),
    )
    return jax.shard_map(
        on_device,
        mesh=mesh,
        in_specs=placed,
        out_specs=(P("inst", "slab", None, None), P("inst", None, "slab")),
        check_vma=False,
    )
```

profile of v0, /device:TPU:1, one launch (start us, length us, event | category | flops | bytes accessed | tf_op | source)
XLA Modules:
  0.0 140.4 jit_solution(3984639888102135299)
XLA Ops:
  7.2 0.0 copy-start
  7.2 0.0 all-gather.2.cloned.1.call-start
  7.2 0.7 all-gather.2.cloned.1.call-update
  7.9 0.5 copy-done
  8.4 4.0 %broadcast_multiply_fusion = (f32[1,8,64,512]{3,2,1,0:T(8,128)S(1)}, f32[1,8,64,512]{3,2,1,0:T(8,128)}, f32[2,8,64,512]{3,2,1,0:T(8,128)S(1)}) fusion(f32[64]{0:T(128)S(1)} %add_multiply_fusion.1, f32[1,8,64,512]{3,2,1,0:T(8,128)} %param.9, f32[1,8,64,512]{3,2,1,0:T(8,128)} %param.8, f32[1,8,64,512]{3,2,1,0:T(8,128)} %param.7, f32[8]{0:T(128)S(1)} %add_multiply_fusion.2, ...), kind=kLoop, calls=%fused_computation.42 | loop fusion | flops 2883583 | bytes 8388896 | tf_op jit(solution)/shard_map/mul | solution.py:89
  12.4 0.0 copy-done.5
  12.4 0.1 constant_dynamic-update-slice_fusion
  12.5 0.0 copy-start.2
  12.5 1.4 copy-done.2
  13.9 0.7 fusion.32
  14.6 4.5 %collective-permute-start = (f32[2,1,64,512]{3,2,1,0:T(8,128)}, f32[2,1,64,512]{3,2,1,0:T(8,128)}, u32[]{:S(2)}, u32[]{:S(2)}) collective-permute-start(f32[2,1,64,512]{3,2,1,0:T(8,128)} %get-tuple-element.7), channel_id=1, source_target_pairs={{0,1},{1,2},{2,3},{3,4},{4,5},{5,6},{6,7},{7,8},{8,9},{9,10},{10,1... | collective-permute-start | bytes 786440 | tf_op jit(solution)/shard_map/ppermute | solution.py:21
  19.1 2.6 %collective-permute-start.1 = (f32[2,1,64,512]{3,2,1,0:T(8,128)S(1)}, f32[2,1,64,512]{3,2,1,0:T(8,128)}, u32[]{:S(2)}, u32[]{:S(2)}) collective-permute-start(f32[2,1,64,512]{3,2,1,0:T(8,128)S(1)} %get-tuple-element.8), channel_id=1, source_target_pairs={{1,0},{2,1},{3,2},{4,3},{5,4},{6,5},{7,6},{8,7},{9,8},{10,9},{11,1... | collective-permute-start | bytes 786440 | tf_op jit(solution)/shard_map/ppermute | solution.py:24
  21.8 0.0 copy-done.8
  21.8 0.6 dynamic-slice
  23.1 0.5 broadcast_compare_fusion.2
  23.5 0.0 copy-start.4
  23.5 2.0 %select_reduce_fusion = (f32[2,512]{1,0:T(2,128)S(1)}, f32[2,512]{1,0:T(2,128)S(1)}, f32[2,512]{1,0:T(2,128)S(1)}) fusion(f32[1,8,64,512]{3,2,1,0:T(8,128)S(1)} %get-tuple-element.5, f32[1,8,64,512]{3,2,1,0:T(8,128)} %get-tuple-element.6, pred[8,64,512]{2,1,0:T(8,128)(4,1)S(1)} %get-tuple-element.10, pred[8,64,512]{2,1,0:T(8,128)(4,1)S(1)} %get-tuple-element.11, ...), kind=kLoop, calls=%fused_computation.6 | loop fusion | flops 3666944 | bytes 2895872 | tf_op jit(solution)/shard_map/reduce_sum | solution.py:97
  25.5 0.3 fusion.18
  25.8 0.3 convolution_add_fusion.1
  26.1 0.3 fusion.12
  26.4 56.2 %all-reduce.4 = f32[2,64]{1,0:T(2,128)S(1)} all-reduce(f32[2,64]{1,0:T(2,128)S(1)} %fusion.12), channel_id=2, replica_groups=mesh['inst'=8,'slab'=32] {'slab'}, use_global_device_ids=true, to_apply=%region_5.6.clone | all-reduce | flops 128 | bytes 1024
  82.6 0.6 dynamic-slice_bitcast_fusion
  83.3 0.4 multiply_add_fusion
  83.7 0.2 select_reduce_fusion.3
  83.9 0.6 copy-done.6
  84.5 1.8 %fusion.3 = f32[8,64,513]{2,1,0:T(8,128)} fusion(f32[8,64,512]{2,1,0:T(8,128)S(1)} %bitcast.18, f32[8,64,512]{2,1,0:T(8,128)S(1)} %bitcast.20), kind=kLoop, calls=%fused_computation.16 | loop fusion | flops 1838592 | bytes 3147776 | tf_op jit(solution)/shard_map/add | solution.py:46
  86.3 0.0 collective-permute-done
  86.3 0.0 collective-permute-done.1
  86.4 1.4 %fusion.10 = f32[1,9,64,512]{3,2,1,0:T(8,128)S(1)} fusion(f32[2,1,64,512]{3,2,1,0:T(8,128)} %collective-permute-done.1, f32[2,8,64,512]{3,2,1,0:T(8,128)S(1)} %copy-done.3, f32[2,1,64,512]{3,2,1,0:T(8,128)} %collective-permute-done), kind=kLoop, calls=%fused_computation.24 | loop fusion | flops 3244032 | bytes 3801088 | tf_op jit(solution)/shard_map/add | solution.py:46
  87.8 39.5 %all-gather.2.cloned.1.call-done = f32[8,8,64,512]{3,2,1,0:T(8,128)} async-done(((f32[1,8,64,512]{3,2,1,0:T(8,128)}), f32[8,8,64,512]{3,2,1,0:T(8,128)}) %all-gather.2.cloned.1.call-update) | async-done | bytes 8388624 | tf_op jit(solution)/shard_map/all_gather | solution.py:69
  127.3 4.7 %multiply_reduce_fusion = f32[8,64,512]{2,1,0:T(8,128)S(1)} fusion(f32[8,8,64,512]{3,2,1,0:T(8,128)} %all-gather.2.cloned.1.call-done, f32[8]{0:T(128)S(1)} %select_reduce_fusion.3), kind=kLoop, calls=%fused_computation | loop fusion | flops 3932160 | bytes 9437216 | tf_op jit(solution)/shard_map/reduce_sum | solution.py:74
  132.0 1.6 %fusion.15 = f32[1,8,64,512]{3,2,1,0:T(8,128)} fusion(f32[8,64,512]{2,1,0:T(8,128)S(1)} %multiply_reduce_fusion, f32[8,64,513]{2,1,0:T(8,128)S(1)} %copy-done.1, f32[8,65,512]{2,1,0:T(8,128)S(1)} %multiply_add_fusion, f32[1,9,64,512]{3,2,1,0:T(8,128)S(1)} %fusion.10), kind=kLoop, calls=%fused_computation.34 | loop fusion | flops 1572864 | bytes 8388608 | tf_op jit(solution)/shard_map/broadcast_in_dim | solution.py:80
  (16 shorter events, 0.1 us)
Async XLA Ops:
  7.2 1.2 copy-start
  7.2 120.1 %all-gather.2.cloned.1.call-start = ((), (), s32[]{:S(2)}) async-start(), calls=%async_computation | async-start | bytes 9437184 | tf_op jit(solution)/shard_map/all_gather | solution.py:69
  8.4 4.0 %copy-start.5 = (f32[1,8,64,512]{3,2,1,0:T(8,128)S(1)}, f32[1,8,64,512]{3,2,1,0:T(8,128)}, u32[]{:S(2)}) copy-start(f32[1,8,64,512]{3,2,1,0:T(8,128)} %param.9) | copy-start | bytes 3145732
  12.4 9.3 %copy-start.8 = (u32[256]{0:T(256)S(1)}, u32[256]{0:T(256)}, u32[]{:S(2)}) copy-start(u32[256]{0:T(256)} %constant.103) | copy-start | bytes 3076
  12.4 10.6 %copy-start.7 = (s32[8,64,512]{2,1,0:T(8,128)S(1)}, s32[8,64,512]{2,1,0:T(8,128)}, u32[]{:S(2)}) copy-start(s32[8,64,512]{2,1,0:T(8,128)} %param.11) | copy-start | bytes 3145732
  12.5 1.4 copy-start.2
  14.6 71.7 %collective-permute-start = (f32[2,1,64,512]{3,2,1,0:T(8,128)}, f32[2,1,64,512]{3,2,1,0:T(8,128)}, u32[]{:S(2)}, u32[]{:S(2)}) collective-permute-start(f32[2,1,64,512]{3,2,1,0:T(8,128)} %get-tuple-element.7), channel_id=1, source_target_pairs={{0,1},{1,2},{2,3},{3,4},{4,5},{5,6},{6,7},{7,8},{8,9},{9,10},{10,1... | collective-permute-start | bytes 786440 | tf_op jit(solution)/shard_map/ppermute | solution.py:21
  19.1 67.2 %collective-permute-start.1 = (f32[2,1,64,512]{3,2,1,0:T(8,128)S(1)}, f32[2,1,64,512]{3,2,1,0:T(8,128)}, u32[]{:S(2)}, u32[]{:S(2)}) collective-permute-start(f32[2,1,64,512]{3,2,1,0:T(8,128)S(1)} %get-tuple-element.8), channel_id=1, source_target_pairs={{1,0},{2,1},{3,2},{4,3},{5,4},{6,5},{7,6},{8,7},{9,8},{10,9},{11,1... | collective-permute-start | bytes 786440 | tf_op jit(solution)/shard_map/ppermute | solution.py:24
  23.5 59.8 %copy-start.4 = (f32[1,8,64,512]{3,2,1,0:T(8,128)S(1)}, f32[1,8,64,512]{3,2,1,0:T(8,128)}, u32[]{:S(2)}) copy-start(f32[1,8,64,512]{3,2,1,0:T(8,128)} %param.8) | copy-start | bytes 3145732
  83.3 1.2 copy-start.6
  84.5 1.8 %copy-start.3 = (f32[2,8,64,512]{3,2,1,0:T(8,128)S(1)}, f32[2,8,64,512]{3,2,1,0:T(8,128)}, u32[]{:S(2)}) copy-start(f32[2,8,64,512]{3,2,1,0:T(8,128)} %copy-done.2) | copy-start | bytes 6291460
  127.3 4.7 %copy-start.1 = (f32[8,64,513]{2,1,0:T(8,128)S(1)}, f32[8,64,513]{2,1,0:T(8,128)}, u32[]{:S(2)}) copy-start(f32[8,64,513]{2,1,0:T(8,128)} %fusion.3) | copy-start | bytes 3151876
Sparse Core Ops, SparseCore 0:
  10.7 116.5 all-gather.1
where the time goes:
time: 141 us; the launch traced here: 140 us
  blocking collectives  56.2 us (40%)
  waiting for transfers between devices  40.2 us (29%)
  other arithmetic  16.7 us (12%)
  between operations  14.8 us (10%)
  starting transfers between devices  7.15 us (5%)
  local copies, waits for them, and re-layouts  4.5 us (3%)
    unnamed x1, blocking collectives  56.2 us
    all_gather x1, waiting for transfers between devices, on_device(): piece = lax.all_gather(volume_frac, 'inst', axis=0, tiled=True)  39.5 us
    reduce_sum x1, other arithmetic, on_device(): derivative = jnp.sum(weights[:, None, None, None] * piece, axis=0)  4.72 us
    ppermute x1, starting transfers between devices, extended(): lax.ppermute(lax.slice_in_dim(block, block.shape[dim] - width, None, axis...  4.5 us
    mul x1, other arithmetic, on_device(): both_loads = jnp.stack([load, load * lever[None, :, None]])  4.02 us
    add x3, other arithmetic, upwind(): jnp.maximum(face_speed, 0.0) * lower_f  3.67 us
    unnamed x19, local copies, waits for them, and re-layouts  3.04 us
  transfers between devices with their start and end apart: 3, of which 1 were waited for; matrix products, arithmetic and copies ran while one was open for 9% of the time, Pallas kernels for 0%

commit v1 on v0

v1 whole, which is shorter than its diff:
```python
import functools
import math

import jax
import jax.numpy as jnp
from jax import lax
from jax.experimental import pallas as pl
from jax.experimental.pallas import tpu as pltpu
from jax.sharding import PartitionSpec as P

MESH = pl.DeviceIdType.MESH
F32 = jnp.float32

GRAVITY = 4.0
SIGMA = 1.0
ROOT2 = math.sqrt(2.0)

CV, NY, NX = 8, 64, 512
N_INST, N_SLAB = 8, 32
NSEC = 64
CHUNKS = 4
ROWS = NY // CHUNKS

PEERS = ((1, 0), (0, 1), (1, 1), (0, 3), (1, 3), (0, 2), (1, 2))
GROUP = ((0, 1), (1, 0), (1, 1))


def flux(speed_lo, speed_hi, lower, upper):
    f = 0.5 * (speed_lo + speed_hi)
    return jnp.maximum(f, 0.0) * lower + jnp.minimum(f, 0.0) * upper


def kernel(vf, vu, vv, vw, wet, sec, res, owned,
           a_s, u_s, v_s, w_s, m_s, s_s, got, ret, back, div, plane, halo, tile, near, far,
           in_sem, p1_send, p1_recv, p2_send, p2_recv, h_send, h_recv, l1_send, l1_recv, l2_send, l2_recv):
    inst = lax.axis_index("inst")
    slab = lax.axis_index("slab")
    xh, y = inst // 4, lax.rem(inst, 4)
    zpos, xl, core = slab // 4, lax.rem(slab // 2, 2), lax.rem(slab, 2)

    def to(dx, dy):
        return lax.rem(xh + dx, 2) * 4 + lax.rem(y + dy, 4)

    def fro(dx, dy):
        return lax.rem(xh + dx, 2) * 4 + lax.rem(y + 4 - dy, 4)

    def grp(dxl, dc):
        return zpos * 4 + lax.rem(xl + dxl, 2) * 2 + lax.rem(core + dc, 2)

    def zto(dz):
        return lax.rem(zpos + dz, N_SLAB // 4) * 4 + xl * 2 + core

    up = lax.rem(slab + 1, N_SLAB)
    down = lax.rem(slab + N_SLAB - 1, N_SLAB)
    n_z = N_SLAB // 4

    barrier = pltpu.get_barrier_semaphore()
    greeted = [(fro(dx, dy), slab) for dx, dy in PEERS]
    greeted += [(inst, up), (inst, down)]
    greeted += [(inst, grp(a, b)) for a, b in GROUP]
    greeted += [(inst, zto(n_z - dz)) for dz in range(1, n_z)]
    for who in greeted:
        pl.semaphore_signal(barrier, inc=1, device_id=who, device_id_type=MESH)

    loads = [
        pltpu.make_async_copy(src.at[0], dst, in_sem.at[i])
        for i, (src, dst) in enumerate(((vf, a_s), (vu, u_s), (vv, v_s), (vw, w_s), (wet, m_s)))
    ]
    loads.append(pltpu.make_async_copy(sec, s_s, in_sem.at[5]))
    for cp in loads:
        cp.start()
    pl.semaphore_wait(barrier, len(greeted))

    def send_out(c, _):
        rows = pl.ds(pl.multiple_of(c * ROWS, ROWS), ROWS)
        for k, (dx, dy) in enumerate(PEERS):
            peer = to(dx, dy)
            pltpu.make_async_remote_copy(
                src_ref=vf.at[0, peer, rows], dst_ref=got.at[c, k],
                send_sem=p1_send, recv_sem=p1_recv.at[c],
                device_id=(peer, slab), device_id_type=MESH,
            ).start()
        return 0

    lax.fori_loop(0, CHUNKS, send_out, 0)

    halo_cps = []
    for side, (who, layer) in enumerate(((up, CV - 1), (down, 0))):
        for q, src in enumerate((vf, vw)):
            halo_cps.append(pltpu.make_async_remote_copy(
                src_ref=src.at[0, layer], dst_ref=halo.at[side, q],
                send_sem=h_send.at[side, q], recv_sem=h_recv.at[side, q],
                device_id=(inst, who), device_id_type=MESH,
            ))
    for cp in halo_cps:
        cp.start()

    for cp in loads:
        cp.wait()

    lane = lax.broadcasted_iota(jnp.int32, (8, NX), 1)
    sub = lax.broadcasted_iota(jnp.int32, (8, NX), 0)
    base = lane // (NX // NSEC)
    total = N_SLAB * CV

    def load_rows(r, sums):
        rows = pl.ds(pl.multiple_of(r * 8, 8), 8)

        def load_layer(v, acc):
            u, vy, w = u_s[v, rows], v_s[v, rows], w_s[v, rows]
            depth = ((slab * CV + v).astype(F32) + 0.5) * (GRAVITY / total)
            pressure = depth + 0.5 * (u * u + vy * vy + w * w)
            load = m_s[v, rows].astype(F32) * a_s[v, rows] * pressure
            rel = s_s[v, rows] - base
            return tuple(a + jnp.where(rel == o, load, 0.0) for a, o in zip(acc, (-1, 0, 1)))

        acc = lax.fori_loop(0, CV, load_layer, (jnp.zeros((8, NX), F32),) * 3)
        lever = ((r * 8 + sub).astype(F32) + 0.5) * (1.0 / NY)
        return tuple(s + a for s, a in zip(sums[:3], acc)) + tuple(s + a * lever for s, a in zip(sums[3:], acc))

    sums = lax.fori_loop(0, NY // 8, load_rows, (jnp.zeros((8, NX), F32),) * 6)
    term = jnp.zeros((16, 128), F32)
    col = lax.broadcasted_iota(jnp.int32, (NX, 128), 0) // (NX // NSEC)
    secs = lax.broadcasted_iota(jnp.int32, (NX, 128), 1)
    for n, o in enumerate((-1, 0, 1)):
        pick = (col + o == secs).astype(F32)
        both = jnp.concatenate([sums[n], sums[3 + n]], axis=0)
        term = term + jnp.dot(both, pick, precision=lax.Precision.HIGHEST, preferred_element_type=F32)
    force = jnp.sum(term[:8], axis=0, keepdims=True)
    moment = jnp.sum(term[8:], axis=0, keepdims=True)
    sub128 = lax.broadcasted_iota(jnp.int32, (8, 128), 0)
    tile[0] = jnp.where(sub128 == 0, force, jnp.where(sub128 == 1, moment, 0.0)) * (2.0 / (CV * NY * NX))
    for k, (a, b) in enumerate(GROUP):
        pltpu.make_async_remote_copy(
            src_ref=tile.at[0], dst_ref=near.at[k], send_sem=l1_send, recv_sem=l1_recv,
            device_id=(inst, grp(a, b)), device_id_type=MESH,
        ).start()

    plane[...] = jnp.zeros_like(plane)
    first_lane, last_lane = lane == 0, lane == NX - 1
    first_sub, last_sub = sub == 0, sub == 7

    def one_layer(v, _):
        above = jnp.minimum(v + 1, CV - 1)
        inner = jnp.where(v < CV - 1, 1.0, 0.0)
        prev = None
        for r in range(NY // 8):
            rows = pl.ds(r * 8, 8)
            a, u, s, w = a_s[v, rows], u_s[v, rows], v_s[v, rows], w_s[v, rows]
            top = flux(w, w_s[above, rows], a, a_s[above, rows]) * inner
            d = top - plane[rows]
            plane[rows] = top
            if r < NY // 8 - 1:
                nxt = pl.ds(r * 8 + 8, 8)
                a_n, s_n = pltpu.roll(a_s[v, nxt], 7, 0), pltpu.roll(v_s[v, nxt], 7, 0)
            else:
                a_n = s_n = jnp.zeros((8, NX), F32)
            a_up = jnp.where(last_sub, a_n, pltpu.roll(a, 7, 0))
            s_up = jnp.where(last_sub, s_n, pltpu.roll(s, 7, 0))
            fy = flux(s, s_up, a, a_up)
            fy_roll = pltpu.roll(fy, 1, 0)
            if prev is None:
                low = jnp.minimum(0.5 * s, 0.0) * a
            else:
                low = prev
            d = d + (fy - jnp.where(first_sub, low, fy_roll))
            prev = fy_roll
            a_r = jnp.where(last_lane, 0.0, pltpu.roll(a, NX - 1, 1))
            u_r = jnp.where(last_lane, 0.0, pltpu.roll(u, NX - 1, 1))
            fx = flux(u, u_r, a, a_r)
            left = jnp.minimum(0.5 * u, 0.0) * a
            d = d + (fx - jnp.where(first_lane, left, pltpu.roll(fx, 1, 1)))
            div[v, rows] = d
        return 0

    lax.fori_loop(0, CV, one_layer, 0)

    pltpu.make_async_copy(near, near, l1_recv).wait()
    tile[1] = tile[0] + near[0] + near[1] + near[2]
    for dz in range(1, n_z):
        pltpu.make_async_remote_copy(
            src_ref=tile.at[1], dst_ref=far.at[dz - 1], send_sem=l2_send, recv_sem=l2_recv,
            device_id=(inst, zto(dz)), device_id_type=MESH,
        ).start()

    sig = [jnp.where(y >= k, 1.0, -1.0) for k in range(4)]
    tau = [jnp.where(y + k < 4, 0.5, -0.5) for k in range(4)]
    slot = {p: k for k, p in enumerate(PEERS)}

    def combine(c, _):
        start = pl.multiple_of(c * ROWS, ROWS)
        pltpu.make_async_copy(got.at[c], got.at[c], p1_recv.at[c]).wait()
        for r in range(ROWS // 8):
            for h in range(2):
                cols = pl.ds(h * 256, 256)
                rr = pl.ds(r * 8, 8)
                p, q = [], []
                for k in range(4):
                    if k == 0:
                        mine = a_s[inst, pl.ds(pl.multiple_of(start + r * 8, 8), 8), cols]
                    else:
                        mine = got[c, slot[(0, k)], rr, cols]
                    other = got[c, slot[(1, k)], rr, cols]
                    p.append(mine + other)
                    q.append((mine - other) * sig[k])
                even, odd = p[0] - p[2], p[3] - p[1]
                nyq = ((p[0] + p[2]) - (p[1] + p[3])) * (SIGMA / N_INST)
                half_odd, half_even = 0.5 * odd, 0.5 * even
                ps = (half_odd + nyq, -half_even - nyq, nyq - half_odd, half_even - nyq)
                qs = (
                    q[2] - ROOT2 * (q[1] + q[3]),
                    q[1] - ROOT2 * (q[0] + q[2]),
                    q[0] - ROOT2 * (q[1] - q[3]),
                    -q[3] - ROOT2 * (q[0] - q[2]),
                )
                for t in range(4):
                    qt = qs[t] * tau[t]
                    if t == 0:
                        back[c, 7, rr, cols] = ps[t] + qt
                    else:
                        ret[c, slot[(0, t)], rr, cols] = ps[t] + qt
                    ret[c, slot[(1, t)], rr, cols] = ps[t] - qt
        for k, (dx, dy) in enumerate(PEERS):
            pltpu.make_async_remote_copy(
                src_ref=ret.at[c, k], dst_ref=back.at[c, k],
                send_sem=p2_send, recv_sem=p2_recv.at[c],
                device_id=(to(dx, dy), slab), device_id_type=MESH,
            ).start()
        return 0

    lax.fori_loop(0, CHUNKS, combine, 0)

    for cp in halo_cps:
        cp.wait()
    keep_lo = jnp.where(slab > 0, 1.0, 0.0)
    keep_hi = jnp.where(slab < N_SLAB - 1, 1.0, 0.0)

    def edges(r, _):
        rows = pl.ds(pl.multiple_of(r * 8, 8), 8)
        lo = flux(halo[0, 1, rows] * keep_lo, w_s[0, rows], halo[0, 0, rows] * keep_lo, a_s[0, rows])
        hi = flux(w_s[CV - 1, rows], halo[1, 1, rows] * keep_hi, a_s[CV - 1, rows], halo[1, 0, rows] * keep_hi)
        div[0, rows] = div[0, rows] - lo
        div[CV - 1, rows] = div[CV - 1, rows] + hi
        return 0

    lax.fori_loop(0, NY // 8, edges, 0)

    pltpu.make_async_copy(far, far, l2_recv).wait()
    whole = tile[1]
    for dz in range(1, n_z):
        whole = whole + far[dz - 1]
    lane128 = lax.broadcasted_iota(jnp.int32, (8, 128), 1)
    for e in range(2):
        one = jnp.sum(jnp.where(lane128 == slab * 2 + e, whole, 0.0), axis=1, keepdims=True)
        owned[0, :, e:e + 1] = one[:2]

    layer_of = [fro(dx, dy) for dx, dy in PEERS] + [inst]

    def finish(c, _):
        start = pl.multiple_of(c * ROWS, ROWS)
        rows = pl.ds(start, ROWS)
        pltpu.make_async_copy(back.at[c, pl.ds(0, 7)], back.at[c, pl.ds(0, 7)], p2_recv.at[c]).wait()
        for k, layer in enumerate(layer_of):
            res[0, layer, rows] = div[layer, rows] + back[c, k]
        return 0

    lax.fori_loop(0, CHUNKS, finish, 0)

    pltpu.make_async_copy(a_s.at[pl.ds(0, 7)], a_s.at[pl.ds(0, 7)], p1_send).wait()
    pltpu.make_async_copy(ret, ret, p2_send).wait()
    pltpu.make_async_copy(near, near, l1_send).wait()
    pltpu.make_async_copy(far, far, l2_send).wait()


def on_device(*args):
    hbm, vmem = pl.BlockSpec(memory_space=pltpu.HBM), pl.BlockSpec(memory_space=pltpu.VMEM)
    block = (CV, NY, NX)
    dma = pltpu.SemaphoreType.DMA
    return pl.pallas_call(
        kernel,
        out_shape=(jax.ShapeDtypeStruct((1,) + block, F32), jax.ShapeDtypeStruct((1, 2, 2), F32)),
        in_specs=[hbm] * 6,
        out_specs=(vmem, vmem),
        scratch_shapes=[
            pltpu.VMEM(block, F32), pltpu.VMEM(block, F32), pltpu.VMEM(block, F32), pltpu.VMEM(block, F32),
            pltpu.VMEM(block, jnp.int32), pltpu.VMEM(block, jnp.int32),
            pltpu.VMEM((CHUNKS, 7, ROWS, NX), F32),
            pltpu.VMEM((CHUNKS, 7, ROWS, NX), F32),
            pltpu.VMEM((CHUNKS, 8, ROWS, NX), F32),
            pltpu.VMEM(block, F32),
            pltpu.VMEM((NY, NX), F32),
            pltpu.VMEM((2, 2, NY, NX), F32),
            pltpu.VMEM((2, 8, 128), F32), pltpu.VMEM((3, 8, 128), F32), pltpu.VMEM((N_SLAB // 4 - 1, 8, 128), F32),
            dma((6,)), dma, dma((CHUNKS,)), dma, dma((CHUNKS,)), dma((2, 2)), dma((2, 2)),
            dma, dma, dma, dma,
        ],
        compiler_params=pltpu.CompilerParams(
            collective_id=0, has_side_effects=True, vmem_limit_bytes=62 << 20
        ),
        cost_estimate=pl.CostEstimate(flops=20_000_000, bytes_accessed=8 << 20, transcendentals=0),
    )(*args)


def solution(mesh):
    placed = (
        P("inst", "slab", None, None),
        P("inst", "slab", None, None),
        P("inst", "slab", None, None),
        P("inst", "slab", None, None),
        P("inst", "slab", None, None),
        P("slab", None, None),
    )
    return jax.shard_map(
        on_device,
        mesh=mesh,
        in_specs=placed,
        out_specs=(P("inst", "slab", None, None), P("inst", None, "slab")),
        check_vma=False,
    )
```

time: 141 us -> 49.4 us (0.35)
  blocking collectives: 56.2 us -> 0 us
  Pallas kernels: 0 us -> 45.8 us
  waiting for transfers between devices: 40.2 us -> 0 us
  other arithmetic: 16.7 us -> 0 us
  between operations: 14.8 us -> 0.65 us
  starting transfers between devices: 7.15 us -> 0 us
  local copies, waits for them, and re-layouts: 4.5 us -> 2.83 us
    unnamed x1 -> x0, blocking collectives: 56.2 us -> none
    pallas_call x0 -> x1, Pallas kernels: none -> 45.8 us  [on_device(): pl.pallas_call(kernel, out_shape=(jax.ShapeDtypeStruct((1,) + block, F32)...]
    all_gather x1 -> x0, waiting for transfers between devices: 39.5 us -> none  [on_device(): piece = lax.all_gather(volume_frac, 'inst', axis=0, tiled=True)]
    ppermute x2 -> x0, starting transfers between devices: 7.11 us -> none  [the longest x1 4.5 us: extended(): lax.ppermute(lax.slice_in_dim(block, block.shape[dim] - width, None, axis...]
    reduce_sum x3 -> x0, other arithmetic: 6.9 us -> none  [the longest x1 4.72 us: on_device(): derivative = jnp.sum(weights[:, None, None, None] * piece, axis=0)]
    mul x2 -> x0, other arithmetic: 4.03 us -> none  [the longest x1 4.02 us: on_device(): both_loads = jnp.stack([load, load * lever[None, :, None]])]
    add x5 -> x0, other arithmetic: 3.73 us -> none  [the longest x3 3.67 us: upwind(): jnp.maximum(face_speed, 0.0) * lower_f]
    broadcast_in_dim x1 -> x0, other arithmetic: 1.58 us -> none  [on_device(): residual = (derivative + divergence)[None]]
  transfers between devices with their start and end apart: 3 -> 0, of which waited for: 1 -> 0; matrix products, arithmetic and copies ran while one was open for 9% -> 0% of each run, Pallas kernels for 0% -> 0%
where the time goes in v1:
time: 49.4 us; the launch traced here: 49.3 us
  Pallas kernels  45.8 us (93%)
  local copies, waits for them, and re-layouts  2.83 us (6%)
  between operations  0.65 us (1%)
    pallas_call x1, Pallas kernels, on_device(): pl.pallas_call(kernel, out_shape=(jax.ShapeDtypeStruct((1,) + block, F32)...  45.8 us
    unnamed x4, local copies, waits for them, and re-layouts  2.83 us

profile of v1, /device:TPU:1, one launch (start us, length us, event | category | flops | bytes accessed | tf_op | source)
XLA Modules:
  0.0 49.3 jit_solution(4314565850245008680)
XLA Ops:
  0.6 45.8 %shard_map.77 = (f32[1,8,64,512]{3,2,1,0:T(8,128)}, f32[1,2,2]{2,1,0:T(2,128)}) custom-call(f32[1,8,64,512]{3,2,1,0:T(8,128)} %vf.1, f32[1,8,64,512]{3,2,1,0:T(8,128)} %vu.1, f32[1,8,64,512]{3,2,1,0:T(8,128)} %vv.1, f32[1,8,64,512]{3,2,1,0:T(8,128)} %vw.1, s32[1,8,64,512]{3,2,1,0:T(8,128)} %wet.1, s32[8,64,512]{2,1,0:T(8,128)} %sec.1), custom_call_target="tpu_custom_call" | custom-call | flops 20000000 | bytes 8388608 | tf_op jit(solution)/shard_map/pallas_call | solution.py:279
  46.5 0.0 copy-start
  46.5 2.3 %copy.10 = f32[1,8,64,512]{3,2,1,0:T(8,128)} copy(f32[1,8,64,512]{3,2,1,0:T(8,128)} %get-tuple-element.4) | data formatting | bytes 2097152
  48.7 0.0 copy-done
  48.7 0.6 %copy.11 = f32[1,2,2]{2,1,0:T(2,128)} copy(f32[1,2,2]{2,1,0:T(2,128)S(1)} %copy-done) | data formatting | bytes 32
Async XLA Ops:
  46.5 2.3 %copy-start = (f32[1,2,2]{2,1,0:T(2,128)S(1)}, f32[1,2,2]{2,1,0:T(2,128)}, u32[]{:S(2)}) copy-start(f32[1,2,2]{2,1,0:T(2,128)} %get-tuple-element.5) | copy-start | bytes 52

commit v2 on v1

--- a/solution.py
+++ b/solution.py
@@ -32,7 +32,7 @@
 
 def kernel(vf, vu, vv, vw, wet, sec, res, owned,
            a_s, u_s, v_s, w_s, m_s, s_s, got, ret, back, div, plane, halo, tile, near, far,
-           in_sem, p1_send, p1_recv, p2_send, p2_recv, h_send, h_recv, l1_send, l1_recv, l2_send, l2_recv):
+           in_sem, p1_send, p1_recv, p2_send, p2_recv, h_send, h_recv, l1_send, l1_recv, l2_send, l2_recv, word):
     inst = lax.axis_index("inst")
     slab = lax.axis_index("slab")
     xh, y = inst // 4, lax.rem(inst, 4)
@@ -44,23 +44,28 @@
     def fro(dx, dy):
         return lax.rem(xh + dx, 2) * 4 + lax.rem(y + 4 - dy, 4)
 
+    def zto(dz):
+        return lax.rem(zpos + dz, n_z) * 4 + xl * 2 + core
+
     def grp(dxl, dc):
         return zpos * 4 + lax.rem(xl + dxl, 2) * 2 + lax.rem(core + dc, 2)
 
-    def zto(dz):
-        return lax.rem(zpos + dz, N_SLAB // 4) * 4 + xl * 2 + core
-
-    up = lax.rem(slab + 1, N_SLAB)
-    down = lax.rem(slab + N_SLAB - 1, N_SLAB)
     n_z = N_SLAB // 4
+    line = ((slab < N_SLAB - 1, slab + 1), (slab > 0, slab - 1))
+    zline = ((zpos < n_z - 1, slab + 4), (zpos > 0, slab - 4))
 
     barrier = pltpu.get_barrier_semaphore()
     greeted = [(fro(dx, dy), slab) for dx, dy in PEERS]
-    greeted += [(inst, up), (inst, down)]
     greeted += [(inst, grp(a, b)) for a, b in GROUP]
-    greeted += [(inst, zto(n_z - dz)) for dz in range(1, n_z)]
+    expected = len(greeted)
     for who in greeted:
         pl.semaphore_signal(barrier, inc=1, device_id=who, device_id_type=MESH)
+    for there, who in line + zline:
+        expected = expected + there.astype(jnp.int32)
+
+        @pl.when(there)
+        def _():
+            pl.semaphore_signal(barrier, inc=1, device_id=(inst, who), device_id_type=MESH)
 
     loads = [
         pltpu.make_async_copy(src.at[0], dst, in_sem.at[i])
@@ -69,7 +74,7 @@
     loads.append(pltpu.make_async_copy(sec, s_s, in_sem.at[5]))
     for cp in loads:
         cp.start()
-    pl.semaphore_wait(barrier, len(greeted))
+    pl.semaphore_wait(barrier, expected)
 
     def send_out(c, _):
         rows = pl.ds(pl.multiple_of(c * ROWS, ROWS), ROWS)
@@ -82,18 +87,29 @@
             ).start()
         return 0
 
-    lax.fori_loop(0, CHUNKS, send_out, 0)
-
-    halo_cps = []
-    for side, (who, layer) in enumerate(((up, CV - 1), (down, 0))):
-        for q, src in enumerate((vf, vw)):
-            halo_cps.append(pltpu.make_async_remote_copy(
-                src_ref=src.at[0, layer], dst_ref=halo.at[side, q],
-                send_sem=h_send.at[side, q], recv_sem=h_recv.at[side, q],
-                device_id=(inst, who), device_id_type=MESH,
-            ))
-    for cp in halo_cps:
-        cp.start()
+    lax.fori_loop(0, CHUNKS // 2, send_out, 0)
+
+    def pass_word(way):
+        @pl.when(zline[1 - way][0])
+        def _():
+            pl.semaphore_wait(word.at[way], 1)
+
+        @pl.when(zline[way][0])
+        def _():
+            pl.semaphore_signal(word.at[way], inc=1, device_id=(inst, zline[way][1]), device_id_type=MESH)
+
+    def spread():
+        for dz in range(1, n_z):
+            pltpu.make_async_remote_copy(
+                src_ref=tile.at[1], dst_ref=far.at[dz - 1], send_sem=l2_send, recv_sem=l2_recv,
+                device_id=(inst, zto(dz)), device_id_type=MESH,
+            ).start()
+
+    pass_word(0)
+
+    @pl.when(zpos >= n_z // 2)
+    def _():
+        pass_word(1)
 
     for cp in loads:
         cp.wait()
@@ -135,6 +151,29 @@
             src_ref=tile.at[0], dst_ref=near.at[k], send_sem=l1_send, recv_sem=l1_recv,
             device_id=(inst, grp(a, b)), device_id_type=MESH,
         ).start()
+
+    lax.fori_loop(CHUNKS // 2, CHUNKS, send_out, 0)
+
+    def halo_copies(side):
+        layer = 0 if side else CV - 1
+        return [
+            pltpu.make_async_remote_copy(
+                src_ref=src.at[0, layer], dst_ref=halo.at[side, q],
+                send_sem=h_send.at[side, q], recv_sem=h_recv.at[side, q],
+                device_id=(inst, line[side][1]), device_id_type=MESH,
+            )
+            for q, src in enumerate((vf, vw))
+        ]
+
+    for side in range(2):
+        @pl.when(line[side][0])
+        def _():
+            for cp in halo_copies(side):
+                cp.start()
+
+        @pl.when(jnp.logical_not(line[1 - side][0]))
+        def _():
+            halo[side] = jnp.zeros((2, NY, NX), F32)
 
     plane[...] = jnp.zeros_like(plane)
     first_lane, last_lane = lane == 0, lane == NX - 1
@@ -177,11 +216,10 @@
 
     pltpu.make_async_copy(near, near, l1_recv).wait()
     tile[1] = tile[0] + near[0] + near[1] + near[2]
-    for dz in range(1, n_z):
-        pltpu.make_async_remote_copy(
-            src_ref=tile.at[1], dst_ref=far.at[dz - 1], send_sem=l2_send, recv_sem=l2_recv,
-            device_id=(inst, zto(dz)), device_id_type=MESH,
-        ).start()
+
+    @pl.when(zpos >= n_z // 2)
+    def _():
+        spread()
 
     sig = [jnp.where(y >= k, 1.0, -1.0) for k in range(4)]
     tau = [jnp.where(y + k < 4, 0.5, -0.5) for k in range(4)]
@@ -230,20 +268,44 @@
 
     lax.fori_loop(0, CHUNKS, combine, 0)
 
-    for cp in halo_cps:
-        cp.wait()
-    keep_lo = jnp.where(slab > 0, 1.0, 0.0)
-    keep_hi = jnp.where(slab < N_SLAB - 1, 1.0, 0.0)
+    @pl.when(zpos < n_z // 2)
+    def _():
+        pass_word(1)
+        spread()
+
+
+    for side in range(2):
+        @pl.when(line[side][0])
+        def _():
+            for cp in halo_copies(side):
+                cp.wait_send()
+
+        @pl.when(line[1 - side][0])
+        def _():
+            for cp in halo_copies(side):
+                cp.wait_recv()
 
     def edges(r, _):
         rows = pl.ds(pl.multiple_of(r * 8, 8), 8)
-        lo = flux(halo[0, 1, rows] * keep_lo, w_s[0, rows], halo[0, 0, rows] * keep_lo, a_s[0, rows])
-        hi = flux(w_s[CV - 1, rows], halo[1, 1, rows] * keep_hi, a_s[CV - 1, rows], halo[1, 0, rows] * keep_hi)
+        lo = flux(halo[0, 1, rows], w_s[0, rows], halo[0, 0, rows], a_s[0, rows])
+        hi = flux(w_s[CV - 1, rows], halo[1, 1, rows], a_s[CV - 1, rows], halo[1, 0, rows])
         div[0, rows] = div[0, rows] - lo
         div[CV - 1, rows] = div[CV - 1, rows] + hi
         return 0
 
     lax.fori_loop(0, NY // 8, edges, 0)
+
+    layer_of = [fro(dx, dy) for dx, dy in PEERS] + [inst]
+
+    def finish(c, _):
+        start = pl.multiple_of(c * ROWS, ROWS)
+        rows = pl.ds(start, ROWS)
+        pltpu.make_async_copy(back.at[c, pl.ds(0, 7)], back.at[c, pl.ds(0, 7)], p2_recv.at[c]).wait()
+        for k, layer in enumerate(layer_of):
+            res[0, layer, rows] = div[layer, rows] + back[c, k]
+        return 0
+
+    lax.fori_loop(0, CHUNKS, finish, 0)
 
     pltpu.make_async_copy(far, far, l2_recv).wait()
     whole = tile[1]
@@ -254,17 +316,6 @@
         one = jnp.sum(jnp.where(lane128 == slab * 2 + e, whole, 0.0), axis=1, keepdims=True)
         owned[0, :, e:e + 1] = one[:2]
 
-    layer_of = [fro(dx, dy) for dx, dy in PEERS] + [inst]
-
-    def finish(c, _):
-        start = pl.multiple_of(c * ROWS, ROWS)
-        rows = pl.ds(start, ROWS)
-        pltpu.make_async_copy(back.at[c, pl.ds(0, 7)], back.at[c, pl.ds(0, 7)], p2_recv.at[c]).wait()
-        for k, layer in enumerate(layer_of):
-            res[0, layer, rows] = div[layer, rows] + back[c, k]
-        return 0
-
-    lax.fori_loop(0, CHUNKS, finish, 0)
 
     pltpu.make_async_copy(a_s.at[pl.ds(0, 7)], a_s.at[pl.ds(0, 7)], p1_send).wait()
     pltpu.make_async_copy(ret, ret, p2_send).wait()
@@ -292,10 +343,10 @@
             pltpu.VMEM((2, 2, NY, NX), F32),
             pltpu.VMEM((2, 8, 128), F32), pltpu.VMEM((3, 8, 128), F32), pltpu.VMEM((N_SLAB // 4 - 1, 8, 128), F32),
             dma((6,)), dma, dma((CHUNKS,)), dma, dma((CHUNKS,)), dma((2, 2)), dma((2, 2)),
-            dma, dma, dma, dma,
+            dma, dma, dma, dma, pltpu.SemaphoreType.REGULAR((2,)),
         ],
         compiler_params=pltpu.CompilerParams(
-            collective_id=0, has_side_effects=True, vmem_limit_bytes=62 << 20
+            collective_id=0, has_side_effects=True, vmem_limit_bytes=52 << 20
         ),
         cost_estimate=pl.CostEstimate(flops=20_000_000, bytes_accessed=8 << 20, transcendentals=0),
     )(*args)

time: 49.4 us -> 41 us (0.83)
  the two profiles are of different devices: /device:TPU:1 before, /device:TPU:129 now
where the time goes in v2:
time: 41 us; the launch traced here: 40.9 us
  Pallas kernels  38.7 us (94%)
  local copies, waits for them, and re-layouts  1.53 us (4%)
  between operations  0.64 us (2%)
    pallas_call x1, Pallas kernels, on_device(): pl.pallas_call(kernel, out_shape=(jax.ShapeDtypeStruct((1,) + block, F32)...  38.7 us
    unnamed x2, local copies, waits for them, and re-layouts  1.53 us

profile of v2, /device:TPU:129, one launch (start us, length us, event | category | flops | bytes accessed | tf_op | source)
XLA Modules:
  0.0 40.9 jit_solution(14444505585230035152)
XLA Ops:
  0.6 38.7 %shard_map.77 = (f32[1,8,64,512]{3,2,1,0:T(8,128)S(1)}, f32[1,2,2]{2,1,0:T(2,128)S(1)}) custom-call(f32[1,8,64,512]{3,2,1,0:T(8,128)} %vf.1, f32[1,8,64,512]{3,2,1,0:T(8,128)} %vu.1, f32[1,8,64,512]{3,2,1,0:T(8,128)} %vv.1, f32[1,8,64,512]{3,2,1,0:T(8,128)} %vw.1, s32[1,8,64,512]{3,2,1,0:T(8,128)} %wet.1, s32[8,64,512]{2,1,0:T(8,128)} %sec.1), custom_call_target="tpu_custom_call" | custom-call | flops 20000000 | bytes 8388608 | tf_op jit(solution)/shard_map/pallas_call | solution.py:330
  39.4 1.0 %copy.10 = f32[1,8,64,512]{3,2,1,0:T(8,128)} copy(f32[1,8,64,512]{3,2,1,0:T(8,128)S(1)} %get-tuple-element.4) | data formatting | bytes 2097152
  40.3 0.6 %copy.11 = f32[1,2,2]{2,1,0:T(2,128)} copy(f32[1,2,2]{2,1,0:T(2,128)S(1)} %get-tuple-element.5) | data formatting | bytes 32

commit v3 on v2

--- a/solution.py
+++ b/solution.py
@@ -18,8 +18,9 @@
 CV, NY, NX = 8, 64, 512
 N_INST, N_SLAB = 8, 32
 NSEC = 64
-CHUNKS = 4
-ROWS = NY // CHUNKS
+STRIP = NY // N_INST
+PARTS = ((1, 3), (4, 3))
+TOP = CV - 1
 
 PEERS = ((1, 0), (0, 1), (1, 1), (0, 3), (1, 3), (0, 2), (1, 2))
 GROUP = ((0, 1), (1, 0), (1, 1))
@@ -31,8 +32,9 @@
 
 
 def kernel(vf, vu, vv, vw, wet, sec, res, owned,
-           a_s, u_s, v_s, w_s, m_s, s_s, got, ret, back, div, plane, halo, tile, near, far,
-           in_sem, p1_send, p1_recv, p2_send, p2_recv, h_send, h_recv, l1_send, l1_recv, l2_send, l2_recv, word):
+           a_s, u_s, v_s, w_s, m_s, s_s, got, ret, back, w_got, j_got, j_ret, div, plane, halo, tile, near, far,
+           in_sem, p1_send, p1_recv, p2_send, p2_recv, first_send, w_send, w_recv, j_send, j_recv, r_send,
+           h_send, h_recv, l1_send, l1_recv, l2_send, l2_recv, word):
     inst = lax.axis_index("inst")
     slab = lax.axis_index("slab")
     xh, y = inst // 4, lax.rem(inst, 4)
@@ -51,8 +53,12 @@
         return zpos * 4 + lax.rem(xl + dxl, 2) * 2 + lax.rem(core + dc, 2)
 
     n_z = N_SLAB // 4
-    line = ((slab < N_SLAB - 1, slab + 1), (slab > 0, slab - 1))
     zline = ((zpos < n_z - 1, slab + 4), (zpos > 0, slab - 4))
+    across = slab + 2 * core - 1
+    paired = jnp.logical_and(across >= 0, across < N_SLAB)
+    joint = jnp.logical_and(core == 1, paired)
+    lent = jnp.logical_and(core == 0, paired)
+    own_first = jnp.logical_not(lent)
 
     barrier = pltpu.get_barrier_semaphore()
     greeted = [(fro(dx, dy), slab) for dx, dy in PEERS]
@@ -60,12 +66,19 @@
     expected = len(greeted)
     for who in greeted:
         pl.semaphore_signal(barrier, inc=1, device_id=who, device_id_type=MESH)
-    for there, who in line + zline:
+    for there, who in zline:
         expected = expected + there.astype(jnp.int32)
 
         @pl.when(there)
         def _():
             pl.semaphore_signal(barrier, inc=1, device_id=(inst, who), device_id_type=MESH)
+
+    expected = expected + N_INST * paired.astype(jnp.int32)
+
+    @pl.when(paired)
+    def _():
+        for n in range(N_INST):
+            pl.semaphore_signal(barrier, inc=1, device_id=(n, across), device_id_type=MESH)
 
     loads = [
         pltpu.make_async_copy(src.at[0], dst, in_sem.at[i])
@@ -76,18 +89,44 @@
         cp.start()
     pl.semaphore_wait(barrier, expected)
 
-    def send_out(c, _):
-        rows = pl.ds(pl.multiple_of(c * ROWS, ROWS), ROWS)
+    def remote(src, dst, send, recv, where):
+        return pltpu.make_async_remote_copy(
+            src_ref=src, dst_ref=dst, send_sem=send, recv_sem=recv, device_id=where, device_id_type=MESH
+        )
+
+    def strip(n):
+        return pl.ds(pl.multiple_of(n * STRIP, STRIP), STRIP)
+
+    def send_out(part, first, count):
+        layers = pl.ds(first, count)
         for k, (dx, dy) in enumerate(PEERS):
             peer = to(dx, dy)
-            pltpu.make_async_remote_copy(
-                src_ref=vf.at[0, peer, rows], dst_ref=got.at[c, k],
-                send_sem=p1_send, recv_sem=p1_recv.at[c],
-                device_id=(peer, slab), device_id_type=MESH,
-            ).start()
-        return 0
-
-    lax.fori_loop(0, CHUNKS // 2, send_out, 0)
+            remote(vf.at[0, layers, strip(peer)], got.at[layers, k], p1_send, p1_recv.at[part], (peer, slab)).start()
+
+    n_parts = len(PARTS)
+    part_top, part_first = n_parts, n_parts + 1
+    everyone = PEERS + ((0, 0),)
+
+    @pl.when(lent)
+    def _():
+        for k, (dx, dy) in enumerate(everyone):
+            peer = to(dx, dy)
+            for q, src in enumerate((vf, vw)):
+                remote(src.at[0, 0, strip(peer)], j_got.at[q, k], j_send, j_recv, (peer, across)).start()
+
+    send_out(0, *PARTS[0])
+    send_out(part_top, TOP, 1)
+
+    @pl.when(joint)
+    def _():
+        for k, (dx, dy) in enumerate(PEERS):
+            peer = to(dx, dy)
+            remote(vw.at[0, TOP, strip(peer)], w_got.at[k], w_send, w_recv, (peer, slab)).start()
+
+    @pl.when(jnp.logical_not(joint))
+    def _():
+        w_got[...] = jnp.zeros_like(w_got)
+        j_got[...] = jnp.zeros_like(j_got)
 
     def pass_word(way):
         @pl.when(zline[1 - way][0])
@@ -152,28 +191,23 @@
             device_id=(inst, grp(a, b)), device_id_type=MESH,
         ).start()
 
-    lax.fori_loop(CHUNKS // 2, CHUNKS, send_out, 0)
-
-    def halo_copies(side):
-        layer = 0 if side else CV - 1
-        return [
-            pltpu.make_async_remote_copy(
-                src_ref=src.at[0, layer], dst_ref=halo.at[side, q],
-                send_sem=h_send.at[side, q], recv_sem=h_recv.at[side, q],
-                device_id=(inst, line[side][1]), device_id_type=MESH,
-            )
-            for q, src in enumerate((vf, vw))
-        ]
-
-    for side in range(2):
-        @pl.when(line[side][0])
-        def _():
-            for cp in halo_copies(side):
-                cp.start()
-
-        @pl.when(jnp.logical_not(line[1 - side][0]))
-        def _():
-            halo[side] = jnp.zeros((2, NY, NX), F32)
+    @pl.when(own_first)
+    def _():
+        for k, (dx, dy) in enumerate(PEERS):
+            peer = to(dx, dy)
+            remote(vf.at[0, 0, strip(peer)], got.at[0, k], first_send, p1_recv.at[part_first], (peer, slab)).start()
+
+    for part in range(1, n_parts):
+        send_out(part, *PARTS[part])
+
+    inner_layer = TOP - TOP * core
+    halo_cps = [
+        remote(src.at[0, inner_layer], halo.at[core, q], h_send.at[q], h_recv.at[q], (inst, slab + 1 - 2 * core))
+        for q, src in enumerate((vf, vw))
+    ]
+    for cp in halo_cps:
+        cp.start()
+    halo[core] = jnp.zeros((2, NY, NX), F32)
 
     plane[...] = jnp.zeros_like(plane)
     first_lane, last_lane = lane == 0, lane == NX - 1
@@ -223,50 +257,102 @@
 
     sig = [jnp.where(y >= k, 1.0, -1.0) for k in range(4)]
     tau = [jnp.where(y + k < 4, 0.5, -0.5) for k in range(4)]
-    slot = {p: k for k, p in enumerate(PEERS)}
-
-    def combine(c, _):
-        start = pl.multiple_of(c * ROWS, ROWS)
-        pltpu.make_async_copy(got.at[c], got.at[c], p1_recv.at[c]).wait()
-        for r in range(ROWS // 8):
-            for h in range(2):
-                cols = pl.ds(h * 256, 256)
-                rr = pl.ds(r * 8, 8)
-                p, q = [], []
-                for k in range(4):
-                    if k == 0:
-                        mine = a_s[inst, pl.ds(pl.multiple_of(start + r * 8, 8), 8), cols]
-                    else:
-                        mine = got[c, slot[(0, k)], rr, cols]
-                    other = got[c, slot[(1, k)], rr, cols]
-                    p.append(mine + other)
-                    q.append((mine - other) * sig[k])
-                even, odd = p[0] - p[2], p[3] - p[1]
-                nyq = ((p[0] + p[2]) - (p[1] + p[3])) * (SIGMA / N_INST)
-                half_odd, half_even = 0.5 * odd, 0.5 * even
-                ps = (half_odd + nyq, -half_even - nyq, nyq - half_odd, half_even - nyq)
-                qs = (
-                    q[2] - ROOT2 * (q[1] + q[3]),
-                    q[1] - ROOT2 * (q[0] + q[2]),
-                    q[0] - ROOT2 * (q[1] - q[3]),
-                    -q[3] - ROOT2 * (q[0] - q[2]),
-                )
-                for t in range(4):
-                    qt = qs[t] * tau[t]
-                    if t == 0:
-                        back[c, 7, rr, cols] = ps[t] + qt
-                    else:
-                        ret[c, slot[(0, t)], rr, cols] = ps[t] + qt
-                    ret[c, slot[(1, t)], rr, cols] = ps[t] - qt
+    slot = {p: k for k, p in enumerate(everyone)}
+    mine = strip(inst)
+
+    def circulant(value):
+        p = [value(0, k) + value(1, k) for k in range(4)]
+        q = [(value(0, k) - value(1, k)) * sig[k] for k in range(4)]
+        half_odd, half_even = 0.5 * (p[3] - p[1]), 0.5 * (p[0] - p[2])
+        nyq = ((p[0] + p[2]) - (p[1] + p[3])) * (SIGMA / N_INST)
+        ps = (half_odd + nyq, -half_even - nyq, nyq - half_odd, half_even - nyq)
+        qs = (
+            q[2] - ROOT2 * (q[1] + q[3]),
+            q[1] - ROOT2 * (q[0] + q[2]),
+            q[0] - ROOT2 * (q[1] - q[3]),
+            -q[3] - ROOT2 * (q[0] - q[2]),
+        )
+        out = {}
+        for t in range(4):
+            qt = qs[t] * tau[t]
+            out[(0, t)] = ps[t] + qt
+            out[(1, t)] = ps[t] - qt
+        return out
+
+    halves = [pl.ds(h * 256, 256) for h in range(2)]
+
+    def arrived(layer, cols):
+        def value(e, k):
+            if (e, k) == (0, 0):
+                return a_s[layer, mine, cols]
+            return got[layer, slot[(e, k)], :, cols]
+
+        return value
+
+    def put(layer, cols, out):
+        for p, value in out.items():
+            if p == (0, 0):
+                back[layer, 7, :, cols] = value
+            else:
+                ret[layer, slot[p], :, cols] = value
+
+    def all_of(ref, sem):
+        pltpu.make_async_copy(ref, ref, sem).wait()
+
+    def one_strip(layer, _):
+        for cols in halves:
+            put(layer, cols, circulant(arrived(layer, cols)))
+        return 0
+
+    def send_back(part, first, count, send):
+        layers = pl.ds(first, count)
         for k, (dx, dy) in enumerate(PEERS):
-            pltpu.make_async_remote_copy(
-                src_ref=ret.at[c, k], dst_ref=back.at[c, k],
-                send_sem=p2_send, recv_sem=p2_recv.at[c],
-                device_id=(to(dx, dy), slab), device_id_type=MESH,
-            ).start()
-        return 0
-
-    lax.fori_loop(0, CHUNKS, combine, 0)
+            remote(ret.at[layers, k], back.at[layers, k], send, p2_recv.at[part], (to(dx, dy), slab)).start()
+
+    def combine(part, first, count):
+        all_of(got.at[pl.ds(first, count)], p1_recv.at[part])
+        lax.fori_loop(first, first + count, one_strip, 0)
+        send_back(part, first, count, p2_send)
+
+    def combine_top():
+        all_of(got.at[TOP], p1_recv.at[part_top])
+
+        @pl.when(joint)
+        def _():
+            all_of(w_got, w_recv)
+            all_of(j_got, j_recv)
+
+        use = jnp.where(joint, 1.0, 0.0)
+        for cols in halves:
+            alpha = arrived(TOP, cols)
+            face = {}
+            for e, k in everyone:
+                w = w_s[TOP, mine, cols] if (e, k) == (0, 0) else w_got[slot[(e, k)], :, cols]
+                n = slot[(e, k)]
+                face[(e, (4 - k) % 4)] = use * flux(w, j_got[1, n, :, cols], alpha(e, k), j_got[0, n, :, cols])
+            out = circulant(alpha)
+            put(TOP, cols, {p: out[p] + face[p] for p in out})
+            out = circulant(lambda e, k: j_got[0, slot[(e, k)], :, cols])
+            for p in out:
+                j_ret[slot[p], :, cols] = out[p] - face[p]
+        send_back(part_top, TOP, 1, p2_send)
+
+        @pl.when(joint)
+        def _():
+            for k, (dx, dy) in enumerate(everyone):
+                remote(j_ret.at[k], back.at[0, k], r_send, p2_recv.at[part_first], (to(dx, dy), across)).start()
+
+    combine(0, *PARTS[0])
+
+    @pl.when(own_first)
+    def _():
+        all_of(got.at[0], p1_recv.at[part_first])
+        one_strip(0, 0)
+        send_back(part_first, 0, 1, first_send)
+
+    for part in range(1, n_parts):
+        combine(part, *PARTS[part])
+    combine_top()
 
     @pl.when(zpos < n_z // 2)
     def _():
@@ -274,38 +360,48 @@
         spread()
 
 
-    for side in range(2):
-        @pl.when(line[side][0])
-        def _():
-            for cp in halo_copies(side):
-                cp.wait_send()
-
-        @pl.when(line[1 - side][0])
-        def _():
-            for cp in halo_copies(side):
-                cp.wait_recv()
+    for cp in halo_cps:
+        cp.wait()
+    use_lo = jnp.where(jnp.logical_or(core == 1, slab == 0), 1.0, 0.0)
+    use_hi = jnp.where(jnp.logical_or(core == 0, slab == N_SLAB - 1), 1.0, 0.0)
 
     def edges(r, _):
         rows = pl.ds(pl.multiple_of(r * 8, 8), 8)
         lo = flux(halo[0, 1, rows], w_s[0, rows], halo[0, 0, rows], a_s[0, rows])
-        hi = flux(w_s[CV - 1, rows], halo[1, 1, rows], a_s[CV - 1, rows], halo[1, 0, rows])
-        div[0, rows] = div[0, rows] - lo
-        div[CV - 1, rows] = div[CV - 1, rows] + hi
+        hi = flux(w_s[TOP, rows], halo[1, 1, rows], a_s[TOP, rows], halo[1, 0, rows])
+        div[0, rows] = div[0, rows] - use_lo * lo
+        div[TOP, rows] = div[TOP, rows] + use_hi * hi
         return 0
 
     lax.fori_loop(0, NY // 8, edges, 0)
 
-    layer_of = [fro(dx, dy) for dx, dy in PEERS] + [inst]
-
-    def finish(c, _):
-        start = pl.multiple_of(c * ROWS, ROWS)
-        rows = pl.ds(start, ROWS)
-        pltpu.make_async_copy(back.at[c, pl.ds(0, 7)], back.at[c, pl.ds(0, 7)], p2_recv.at[c]).wait()
-        for k, layer in enumerate(layer_of):
-            res[0, layer, rows] = div[layer, rows] + back[c, k]
+    home = [strip(fro(dx, dy)) for dx, dy in everyone]
+
+    def finish(layer, _):
+        for k, rows in enumerate(home):
+            res[0, layer, rows] = div[layer, rows] + back[layer, k]
         return 0
 
-    lax.fori_loop(0, CHUNKS, finish, 0)
+    def finish_part(part, first, count):
+        theirs = back.at[pl.ds(first, count), pl.ds(0, 7)]
+        all_of(theirs, p2_recv.at[part])
+        lax.fori_loop(first, first + count, finish, 0)
+
+    finish_part(0, *PARTS[0])
+
+    for part in range(1, n_parts):
+        finish_part(part, *PARTS[part])
+    finish_part(part_top, TOP, 1)
+
+    @pl.when(lent)
+    def _():
+        all_of(back.at[0], p2_recv.at[part_first])
+
+    @pl.when(own_first)
+    def _():
+        all_of(back.at[0, pl.ds(0, 7)], p2_recv.at[part_first])
+
+    finish(0, 0)
 
     pltpu.make_async_copy(far, far, l2_recv).wait()
     whole = tile[1]
@@ -316,9 +412,22 @@
         one = jnp.sum(jnp.where(lane128 == slab * 2 + e, whole, 0.0), axis=1, keepdims=True)
         owned[0, :, e:e + 1] = one[:2]
 
-
-    pltpu.make_async_copy(a_s.at[pl.ds(0, 7)], a_s.at[pl.ds(0, 7)], p1_send).wait()
-    pltpu.make_async_copy(ret, ret, p2_send).wait()
+    all_of(got.at[pl.ds(1, CV - 1)], p1_send)
+    all_of(ret.at[pl.ds(1, CV - 1)], p2_send)
+
+    @pl.when(own_first)
+    def _():
+        all_of(got.at[pl.ds(0, 2)], first_send)
+
+    @pl.when(lent)
+    def _():
+        all_of(j_got, j_send)
+
+    @pl.when(joint)
+    def _():
+        all_of(w_got, w_send)
+        all_of(j_ret, r_send)
+
     pltpu.make_async_copy(near, near, l1_send).wait()
     pltpu.make_async_copy(far, far, l2_send).wait()
 
@@ -335,14 +444,16 @@
         scratch_shapes=[
             pltpu.VMEM(block, F32), pltpu.VMEM(block, F32), pltpu.VMEM(block, F32), pltpu.VMEM(block, F32),
             pltpu.VMEM(block, jnp.int32), pltpu.VMEM(block, jnp.int32),
-            pltpu.VMEM((CHUNKS, 7, ROWS, NX), F32),
-            pltpu.VMEM((CHUNKS, 7, ROWS, NX), F32),
-            pltpu.VMEM((CHUNKS, 8, ROWS, NX), F32),
+            pltpu.VMEM((CV, 7, STRIP, NX), F32),
+            pltpu.VMEM((CV, 7, STRIP, NX), F32),
+            pltpu.VMEM((CV, 8, STRIP, NX), F32),
+            pltpu.VMEM((7, STRIP, NX), F32), pltpu.VMEM((2, 8, STRIP, NX), F32), pltpu.VMEM((8, STRIP, NX), F32),
             pltpu.VMEM(block, F32),
             pltpu.VMEM((NY, NX), F32),
             pltpu.VMEM((2, 2, NY, NX), F32),
             pltpu.VMEM((2, 8, 128), F32), pltpu.VMEM((3, 8, 128), F32), pltpu.VMEM((N_SLAB // 4 - 1, 8, 128), F32),
-            dma((6,)), dma, dma((CHUNKS,)), dma, dma((CHUNKS,)), dma((2, 2)), dma((2, 2)),
+            dma((6,)), dma, dma((len(PARTS) + 2,)), dma, dma((len(PARTS) + 2,)), dma, dma, dma, dma, dma, dma,
+            dma((2,)), dma((2,)),
             dma, dma, dma, dma, pltpu.SemaphoreType.REGULAR((2,)),
         ],
         compiler_params=pltpu.CompilerParams(

time: 41 us -> 40 us (0.976)
  the two profiles are of different devices: /device:TPU:129 before, /device:TPU:225 now
where the time goes in v3:
time: 40 us; the launch traced here: 39.9 us
  Pallas kernels  37.8 us (94%)
  local copies, waits for them, and re-layouts  1.53 us (4%)
  between operations  0.64 us (2%)
    pallas_call x1, Pallas kernels, on_device(): pl.pallas_call(kernel, out_shape=(jax.ShapeDtypeStruct((1,) + block, F32)...  37.8 us
    unnamed x2, local copies, waits for them, and re-layouts  1.53 us

profile of v3, /device:TPU:225, one launch (start us, length us, event | category | flops | bytes accessed | tf_op | source)
XLA Modules:
  0.0 39.9 jit_solution(1106446092891800866)
XLA Ops:
  0.6 37.8 %shard_map.77 = (f32[1,8,64,512]{3,2,1,0:T(8,128)S(1)}, f32[1,2,2]{2,1,0:T(2,128)S(1)}) custom-call(f32[1,8,64,512]{3,2,1,0:T(8,128)} %vf.1, f32[1,8,64,512]{3,2,1,0:T(8,128)} %vu.1, f32[1,8,64,512]{3,2,1,0:T(8,128)} %vv.1, f32[1,8,64,512]{3,2,1,0:T(8,128)} %vw.1, s32[1,8,64,512]{3,2,1,0:T(8,128)} %wet.1, s32[8,64,512]{2,1,0:T(8,128)} %sec.1), custom_call_target="tpu_custom_call" | custom-call | flops 20000000 | bytes 8388608 | tf_op jit(solution)/shard_map/pallas_call | solution.py:439
  38.4 1.0 %copy.10 = f32[1,8,64,512]{3,2,1,0:T(8,128)} copy(f32[1,8,64,512]{3,2,1,0:T(8,128)S(1)} %get-tuple-element.4) | data formatting | bytes 2097152
  39.4 0.6 %copy.11 = f32[1,2,2]{2,1,0:T(2,128)} copy(f32[1,2,2]{2,1,0:T(2,128)S(1)} %get-tuple-element.5) | data formatting | bytes 32

commit v4 on v3

--- a/solution.py
+++ b/solution.py
@@ -32,8 +32,8 @@
 
 
 def kernel(vf, vu, vv, vw, wet, sec, res, owned,
-           a_s, u_s, v_s, w_s, m_s, s_s, got, ret, back, w_got, j_got, j_ret, div, plane, halo, tile, near, far,
-           in_sem, p1_send, p1_recv, p2_send, p2_recv, first_send, w_send, w_recv, j_send, j_recv, r_send,
+           a_s, u_s, v_s, w_s, m_s, s_s, got, ret, back, w_got, j_got, j_ret, relay, relay_f, div, plane, halo, tile, near, far,
+           in_sem, p1_send, p1_recv, p2_send, p2_recv, first_send, w_send, w_recv, j_send, j_recv, f_send, f_recv, r_send,
            h_send, h_recv, l1_send, l1_recv, l2_send, l2_recv, word):
     inst = lax.axis_index("inst")
     slab = lax.axis_index("slab")
@@ -59,6 +59,7 @@
     joint = jnp.logical_and(core == 1, paired)
     lent = jnp.logical_and(core == 0, paired)
     own_first = jnp.logical_not(lent)
+    flat = core != xl
 
     barrier = pltpu.get_barrier_semaphore()
     greeted = [(fro(dx, dy), slab) for dx, dy in PEERS]
@@ -106,27 +107,56 @@
     n_parts = len(PARTS)
     part_top, part_first = n_parts, n_parts + 1
     everyone = PEERS + ((0, 0),)
-
-    @pl.when(lent)
-    def _():
-        for k, (dx, dy) in enumerate(everyone):
+    slot = {p: k for k, p in enumerate(everyone)}
+
+    half = pl.ds(pl.multiple_of((1 - xh) * (NY // 2), NY // 2), NY // 2)
+    same_half = ((0, 0), (0, 1), (0, 3), (0, 2))
+
+    other_half = tuple((1, k) for k in range(4))
+
+    def lend(pairs):
+        for dx, dy in pairs:
             peer = to(dx, dy)
             for q, src in enumerate((vf, vw)):
-                remote(src.at[0, 0, strip(peer)], j_got.at[q, k], j_send, j_recv, (peer, across)).start()
+                remote(src.at[0, 0, strip(peer)], j_got.at[q, slot[(dx, dy)]], j_send, j_recv, (peer, across)).start()
+
+    @pl.when(jnp.logical_and(lent, flat))
+    def _():
+        for q, src in enumerate((vf, vw)):
+            remote(src.at[0, 0, half], relay.at[q], j_send, f_recv, (inst, across)).start()
+
+    @pl.when(jnp.logical_and(lent, jnp.logical_not(flat)))
+    def _():
+        lend(other_half)
+
+    @pl.when(lent)
+    def _():
+        lend(same_half)
 
     send_out(0, *PARTS[0])
     send_out(part_top, TOP, 1)
 
+    def send_w(pairs, n):
+        for k, (dx, dy) in enumerate(pairs):
+            peer = to(dx, dy)
+            remote(vw.at[0, TOP, strip(peer)], w_got.at[3 * n + k], w_send.at[n], w_recv.at[n], (peer, slab)).start()
+
     @pl.when(joint)
     def _():
-        for k, (dx, dy) in enumerate(PEERS):
-            peer = to(dx, dy)
-            remote(vw.at[0, TOP, strip(peer)], w_got.at[k], w_send, w_recv, (peer, slab)).start()
+        send_w(same_half[1:], 0)
+
+    @pl.when(jnp.logical_and(joint, jnp.logical_not(flat)))
+    def _():
+        send_w(other_half, 1)
 
     @pl.when(jnp.logical_not(joint))
     def _():
-        w_got[...] = jnp.zeros_like(w_got)
+        w_got[0:3] = jnp.zeros((3, STRIP, NX), F32)
         j_got[...] = jnp.zeros_like(j_got)
+
+    @pl.when(jnp.logical_or(jnp.logical_not(joint), flat))
+    def _():
+        w_got[3:7] = jnp.zeros((4, STRIP, NX), F32)
 
     def pass_word(way):
         @pl.when(zline[1 - way][0])
@@ -190,6 +220,16 @@
             src_ref=tile.at[0], dst_ref=near.at[k], send_sem=l1_send, recv_sem=l1_recv,
             device_id=(inst, grp(a, b)), device_id_type=MESH,
         ).start()
+
+    @pl.when(jnp.logical_and(joint, flat))
+    def _():
+        pltpu.make_async_copy(relay, relay, f_recv).wait()
+        relay_f[...] = flux(w_s[TOP, half], relay[1], a_s[TOP, half], relay[0])
+        for k in range(4):
+            peer = to(1, k)
+            rows = strip(lax.rem(peer, 4))
+            for q, src in enumerate((relay.at[0], relay_f)):
+                remote(src.at[rows], j_got.at[q, slot[(1, k)]], f_send, j_recv, (peer, slab)).start()
 
     @pl.when(own_first)
     def _():
@@ -257,7 +297,6 @@
 
     sig = [jnp.where(y >= k, 1.0, -1.0) for k in range(4)]
     tau = [jnp.where(y + k < 4, 0.5, -0.5) for k in range(4)]
-    slot = {p: k for k, p in enumerate(everyone)}
     mine = strip(inst)
 
     def circulant(value):
@@ -319,17 +358,27 @@
 
         @pl.when(joint)
         def _():
-            all_of(w_got, w_recv)
+            all_of(w_got.at[pl.ds(0, 3)], w_recv.at[0])
             all_of(j_got, j_recv)
+
+        @pl.when(jnp.logical_and(joint, jnp.logical_not(flat)))
+        def _():
+            all_of(w_got.at[pl.ds(3, 4)], w_recv.at[1])
 
         use = jnp.where(joint, 1.0, 0.0)
         for cols in halves:
             alpha = arrived(TOP, cols)
             face = {}
             for e, k in everyone:
-                w = w_s[TOP, mine, cols] if (e, k) == (0, 0) else w_got[slot[(e, k)], :, cols]
                 n = slot[(e, k)]
-                face[(e, (4 - k) % 4)] = use * flux(w, j_got[1, n, :, cols], alpha(e, k), j_got[0, n, :, cols])
+                if n == 7:
+                    w = w_s[TOP, mine, cols]
+                else:
+                    w = w_got[3 + k if e else same_half.index((e, k)) - 1, :, cols]
+                f = flux(w, j_got[1, n, :, cols], alpha(e, k), j_got[0, n, :, cols])
+                if e:
+                    f = jnp.where(flat, j_got[1, n, :, cols], f)
+                face[(e, (4 - k) % 4)] = use * f
             out = circulant(alpha)
             put(TOP, cols, {p: out[p] + face[p] for p in out})
             out = circulant(lambda e, k: j_got[0, slot[(e, k)], :, cols])
@@ -425,8 +474,16 @@
 
     @pl.when(joint)
     def _():
-        all_of(w_got, w_send)
+        all_of(w_got.at[pl.ds(0, 3)], w_send.at[0])
         all_of(j_ret, r_send)
+
+    @pl.when(jnp.logical_and(joint, flat))
+    def _():
+        all_of(j_ret, f_send)
+
+    @pl.when(jnp.logical_and(joint, jnp.logical_not(flat)))
+    def _():
+        all_of(w_got.at[pl.ds(3, 4)], w_send.at[1])
 
     pltpu.make_async_copy(near, near, l1_send).wait()
     pltpu.make_async_copy(far, far, l2_send).wait()
@@ -448,11 +505,12 @@
             pltpu.VMEM((CV, 7, STRIP, NX), F32),
             pltpu.VMEM((CV, 8, STRIP, NX), F32),
             pltpu.VMEM((7, STRIP, NX), F32), pltpu.VMEM((2, 8, STRIP, NX), F32), pltpu.VMEM((8, STRIP, NX), F32),
+            pltpu.VMEM((2, NY // 2, NX), F32), pltpu.VMEM((NY // 2, NX), F32),
             pltpu.VMEM(block, F32),
             pltpu.VMEM((NY, NX), F32),
             pltpu.VMEM((2, 2, NY, NX), F32),
             pltpu.VMEM((2, 8, 128), F32), pltpu.VMEM((3, 8, 128), F32), pltpu.VMEM((N_SLAB // 4 - 1, 8, 128), F32),
-            dma((6,)), dma, dma((len(PARTS) + 2,)), dma, dma((len(PARTS) + 2,)), dma, dma, dma, dma, dma, dma,
+            dma((6,)), dma, dma((len(PARTS) + 2,)), dma, dma((len(PARTS) + 2,)), dma, dma((2,)), dma((2,)), dma, dma, dma, dma, dma,
             dma((2,)), dma((2,)),
             dma, dma, dma, dma, pltpu.SemaphoreType.REGULAR((2,)),
         ],

time: 40 us -> 38.1 us (0.953)
  the two profiles are of different devices: /device:TPU:225 before, /device:TPU:1 now
where the time goes in v4:
time: 38.1 us; the launch traced here: 37.6 us
  Pallas kernels  35.5 us (93%)
  local copies, waits for them, and re-layouts  1.53 us (4%)
  between operations  0.64 us (2%)
    pallas_call x1, Pallas kernels, on_device(): pl.pallas_call(kernel, out_shape=(jax.ShapeDtypeStruct((1,) + block, F32)...  35.5 us
    unnamed x2, local copies, waits for them, and re-layouts  1.53 us

profile of v4, /device:TPU:1, one launch (start us, length us, event | category | flops | bytes accessed | tf_op | source)
XLA Modules:
  0.0 37.6 jit_solution(10519382623721987892)
XLA Ops:
  0.6 35.5 %shard_map.77 = (f32[1,8,64,512]{3,2,1,0:T(8,128)S(1)}, f32[1,2,2]{2,1,0:T(2,128)S(1)}) custom-call(f32[1,8,64,512]{3,2,1,0:T(8,128)} %vf.1, f32[1,8,64,512]{3,2,1,0:T(8,128)} %vu.1, f32[1,8,64,512]{3,2,1,0:T(8,128)} %vv.1, f32[1,8,64,512]{3,2,1,0:T(8,128)} %vw.1, s32[1,8,64,512]{3,2,1,0:T(8,128)} %wet.1, s32[8,64,512]{2,1,0:T(8,128)} %sec.1), custom_call_target="tpu_custom_call" | custom-call | flops 20000000 | bytes 8388608 | tf_op jit(solution)/shard_map/pallas_call | solution.py:496
  36.1 1.0 %copy.10 = f32[1,8,64,512]{3,2,1,0:T(8,128)} copy(f32[1,8,64,512]{3,2,1,0:T(8,128)S(1)} %get-tuple-element.4) | data formatting | bytes 2097152
  37.1 0.6 %copy.11 = f32[1,2,2]{2,1,0:T(2,128)} copy(f32[1,2,2]{2,1,0:T(2,128)S(1)} %get-tuple-element.5) | data formatting | bytes 32

commit v5 on v4

--- a/solution.py
+++ b/solution.py
@@ -22,7 +22,7 @@
 PARTS = ((1, 3), (4, 3))
 TOP = CV - 1
 
-PEERS = ((1, 0), (0, 1), (1, 1), (0, 3), (1, 3), (0, 2), (1, 2))
+PEERS = ((1, 2), (1, 1), (1, 3), (1, 0), (0, 2), (0, 1), (0, 3))
 GROUP = ((0, 1), (1, 0), (1, 1))
 
 
@@ -489,11 +489,21 @@
     pltpu.make_async_copy(far, far, l2_send).wait()
 
 
+def hand_over(res, owned, res_out, owned_out, sem):
+    copies = [
+        pltpu.make_async_copy(src, dst, sem.at[n]) for n, (src, dst) in enumerate(((res, res_out), (owned, owned_out)))
+    ]
+    for cp in copies:
+        cp.start()
+    for cp in copies:
+        cp.wait()
+
+
 def on_device(*args):
     hbm, vmem = pl.BlockSpec(memory_space=pltpu.HBM), pl.BlockSpec(memory_space=pltpu.VMEM)
     block = (CV, NY, NX)
     dma = pltpu.SemaphoreType.DMA
-    return pl.pallas_call(
+    made = pl.pallas_call(
         kernel,
         out_shape=(jax.ShapeDtypeStruct((1,) + block, F32), jax.ShapeDtypeStruct((1, 2, 2), F32)),
         in_specs=[hbm] * 6,
@@ -519,6 +529,14 @@
         ),
         cost_estimate=pl.CostEstimate(flops=20_000_000, bytes_accessed=8 << 20, transcendentals=0),
     )(*args)
+    return pl.pallas_call(
+        hand_over,
+        out_shape=tuple(jax.ShapeDtypeStruct(m.shape, F32) for m in made),
+        in_specs=[vmem, vmem],
+        out_specs=(hbm, hbm),
+        scratch_shapes=[dma((2,))],
+        compiler_params=pltpu.CompilerParams(vmem_limit_bytes=1 << 20),
+    )(*made)
 
 
 def solution(mesh):

time: 38.1 us -> 37 us (0.971)
  local copies, waits for them, and re-layouts: 1.53 us -> 0 us
    unnamed x2 -> x0, local copies, waits for them, and re-layouts: 1.53 us -> none
    pallas_call x0 -> x1, Pallas kernels: none -> 0.99 us  [on_device(): pl.pallas_call(hand_over, out_shape=tuple((jax.ShapeDtypeStruct(m.shape,...]
    pallas_call x1, Pallas kernels: 35.5 us -> 34.7 us  [on_device(): pl.pallas_call(kernel, out_shape=(jax.ShapeDtypeStruct((1,) + block, F32)...]
where the time goes in v5:
time: 37 us; the launch traced here: 36.4 us
  Pallas kernels  35.7 us (96%)
  between operations  0.64 us (2%)
    pallas_call x1, Pallas kernels, on_device(): pl.pallas_call(kernel, out_shape=(jax.ShapeDtypeStruct((1,) + block, F32)...  34.7 us
    pallas_call x1, Pallas kernels, on_device(): pl.pallas_call(hand_over, out_shape=tuple((jax.ShapeDtypeStruct(m.shape,...  0.99 us

profile of v5, /device:TPU:1, one launch (start us, length us, event | category | flops | bytes accessed | tf_op | source)
XLA Modules:
  0.0 36.4 jit_solution(16470442154566896206)
XLA Ops:
  0.6 34.7 %shard_map.77 = (f32[1,8,64,512]{3,2,1,0:T(8,128)S(1)}, f32[1,2,2]{2,1,0:T(2,128)S(1)}) custom-call(f32[1,8,64,512]{3,2,1,0:T(8,128)} %vf.1, f32[1,8,64,512]{3,2,1,0:T(8,128)} %vu.1, f32[1,8,64,512]{3,2,1,0:T(8,128)} %vv.1, f32[1,8,64,512]{3,2,1,0:T(8,128)} %vw.1, s32[1,8,64,512]{3,2,1,0:T(8,128)} %wet.1, s32[8,64,512]{2,1,0:T(8,128)} %sec.1), custom_call_target="tpu_custom_call" | custom-call | flops 20000000 | bytes 8388608 | tf_op jit(solution)/shard_map/pallas_call | solution.py:506
  35.4 1.0 %shard_map.78 = (f32[1,8,64,512]{3,2,1,0:T(8,128)}, f32[1,2,2]{2,1,0:T(2,128)}) custom-call(f32[1,8,64,512]{3,2,1,0:T(8,128)S(1)} %get-tuple-element.4.res, f32[1,2,2]{2,1,0:T(2,128)S(1)} %get-tuple-element.5.owned), custom_call_target="tpu_custom_call" | custom-call | tf_op jit(solution)/shard_map/pallas_call | solution.py:532

commit v6 on v5

--- a/solution.py
+++ b/solution.py
@@ -182,6 +182,16 @@
 
     for cp in loads:
         cp.wait()
+
+    @pl.when(jnp.logical_and(joint, flat))
+    def _():
+        pltpu.make_async_copy(relay, relay, f_recv).wait()
+        relay_f[...] = flux(w_s[TOP, half], relay[1], a_s[TOP, half], relay[0])
+        for k in range(4):
+            peer = to(1, k)
+            rows = strip(lax.rem(peer, 4))
+            for q, src in enumerate((relay.at[0], relay_f)):
+                remote(src.at[rows], j_got.at[q, slot[(1, k)]], f_send, j_recv, (peer, slab)).start()
 
     lane = lax.broadcasted_iota(jnp.int32, (8, NX), 1)
     sub = lax.broadcasted_iota(jnp.int32, (8, NX), 0)
@@ -220,16 +230,6 @@
             src_ref=tile.at[0], dst_ref=near.at[k], send_sem=l1_send, recv_sem=l1_recv,
             device_id=(inst, grp(a, b)), device_id_type=MESH,
         ).start()
-
-    @pl.when(jnp.logical_and(joint, flat))
-    def _():
-        pltpu.make_async_copy(relay, relay, f_recv).wait()
-        relay_f[...] = flux(w_s[TOP, half], relay[1], a_s[TOP, half], relay[0])
-        for k in range(4):
-            peer = to(1, k)
-            rows = strip(lax.rem(peer, 4))
-            for q, src in enumerate((relay.at[0], relay_f)):
-                remote(src.at[rows], j_got.at[q, slot[(1, k)]], f_send, j_recv, (peer, slab)).start()
 
     @pl.when(own_first)
     def _():
@@ -440,17 +440,6 @@
 
     for part in range(1, n_parts):
         finish_part(part, *PARTS[part])
-    finish_part(part_top, TOP, 1)
-
-    @pl.when(lent)
-    def _():
-        all_of(back.at[0], p2_recv.at[part_first])
-
-    @pl.when(own_first)
-    def _():
-        all_of(back.at[0, pl.ds(0, 7)], p2_recv.at[part_first])
-
-    finish(0, 0)
 
     pltpu.make_async_copy(far, far, l2_recv).wait()
     whole = tile[1]
@@ -460,6 +449,18 @@
     for e in range(2):
         one = jnp.sum(jnp.where(lane128 == slab * 2 + e, whole, 0.0), axis=1, keepdims=True)
         owned[0, :, e:e + 1] = one[:2]
+
+    finish_part(part_top, TOP, 1)
+
+    @pl.when(lent)
+    def _():
+        all_of(back.at[0], p2_recv.at[part_first])
+
+    @pl.when(own_first)
+    def _():
+        all_of(back.at[0, pl.ds(0, 7)], p2_recv.at[part_first])
+
+    finish(0, 0)
 
     all_of(got.at[pl.ds(1, CV - 1)], p1_send)
     all_of(ret.at[pl.ds(1, CV - 1)], p2_send)

time: 37 us -> 37 us (level)
  no operation moved by 1% of the time
where the time goes in v6:
time: 37 us; the launch traced here: 36.3 us
  Pallas kernels  35.6 us (96%)
  between operations  0.64 us (2%)
    pallas_call x1, Pallas kernels, on_device(): pl.pallas_call(kernel, out_shape=(jax.ShapeDtypeStruct((1,) + block, F32)...  34.6 us
    pallas_call x1, Pallas kernels, on_device(): pl.pallas_call(hand_over, out_shape=tuple((jax.ShapeDtypeStruct(m.shape,...  0.99 us

profile of v6, /device:TPU:1, one launch (start us, length us, event | category | flops | bytes accessed | tf_op | source)
XLA Modules:
  0.0 36.3 jit_solution(10007663702588203574)
XLA Ops:
  0.6 34.6 %shard_map.77 = (f32[1,8,64,512]{3,2,1,0:T(8,128)S(1)}, f32[1,2,2]{2,1,0:T(2,128)S(1)}) custom-call(f32[1,8,64,512]{3,2,1,0:T(8,128)} %vf.1, f32[1,8,64,512]{3,2,1,0:T(8,128)} %vu.1, f32[1,8,64,512]{3,2,1,0:T(8,128)} %vv.1, f32[1,8,64,512]{3,2,1,0:T(8,128)} %vw.1, s32[1,8,64,512]{3,2,1,0:T(8,128)} %wet.1, s32[8,64,512]{2,1,0:T(8,128)} %sec.1), custom_call_target="tpu_custom_call" | custom-call | flops 20000000 | bytes 8388608 | tf_op jit(solution)/shard_map/pallas_call | solution.py:507
  35.3 1.0 %shard_map.78 = (f32[1,8,64,512]{3,2,1,0:T(8,128)}, f32[1,2,2]{2,1,0:T(2,128)}) custom-call(f32[1,8,64,512]{3,2,1,0:T(8,128)S(1)} %get-tuple-element.4.res, f32[1,2,2]{2,1,0:T(2,128)S(1)} %get-tuple-element.5.owned), custom_call_target="tpu_custom_call" | custom-call | tf_op jit(solution)/shard_map/pallas_call | solution.py:533

commit v7 on v6

--- a/solution.py
+++ b/solution.py
@@ -32,9 +32,9 @@
 
 
 def kernel(vf, vu, vv, vw, wet, sec, res, owned,
-           a_s, u_s, v_s, w_s, m_s, s_s, got, ret, back, w_got, j_got, j_ret, relay, relay_f, div, plane, halo, tile, near, far,
+           a_s, u_s, v_s, w_s, m_s, s_s, got, ret, back, w_got, j_got, j_ret, relay, relay_f, div, plane, halo, tile, near, far, summed,
            in_sem, p1_send, p1_recv, p2_send, p2_recv, first_send, w_send, w_recv, j_send, j_recv, f_send, f_recv, r_send,
-           h_send, h_recv, l1_send, l1_recv, l2_send, l2_recv, word):
+           h_send, h_recv, l1_send, l1_recv, l2_send, l2_recv, t_send, t_recv, word):
     inst = lax.axis_index("inst")
     slab = lax.axis_index("slab")
     xh, y = inst // 4, lax.rem(inst, 4)
@@ -53,7 +53,11 @@
         return zpos * 4 + lax.rem(xl + dxl, 2) * 2 + lax.rem(core + dc, 2)
 
     n_z = N_SLAB // 4
-    zline = ((zpos < n_z - 1, slab + 4), (zpos > 0, slab - 4))
+    leader = lax.rem(slab, 4) == 3
+    zline = (
+        (jnp.logical_and(leader, zpos < n_z - 1), slab + 4),
+        (jnp.logical_and(leader, zpos > 0), slab - 4),
+    )
     across = slab + 2 * core - 1
     paired = jnp.logical_and(across >= 0, across < N_SLAB)
     joint = jnp.logical_and(core == 1, paired)
@@ -291,7 +295,7 @@
     pltpu.make_async_copy(near, near, l1_recv).wait()
     tile[1] = tile[0] + near[0] + near[1] + near[2]
 
-    @pl.when(zpos >= n_z // 2)
+    @pl.when(jnp.logical_and(leader, zpos >= n_z // 2))
     def _():
         spread()
 
@@ -403,7 +407,7 @@
         combine(part, *PARTS[part])
     combine_top()
 
-    @pl.when(zpos < n_z // 2)
+    @pl.when(jnp.logical_and(leader, zpos < n_z // 2))
     def _():
         pass_word(1)
         spread()
@@ -438,30 +442,41 @@
 
     finish_part(0, *PARTS[0])
 
+    @pl.when(leader)
+    def _():
+        all_of(far, l2_recv)
+        whole = tile[1]
+        for dz in range(1, n_z):
+            whole = whole + far[dz - 1]
+        summed[...] = whole
+        for p, q in GROUP:
+            remote(summed, summed, t_send, t_recv, (inst, grp(p, q))).start()
+
     for part in range(1, n_parts):
         finish_part(part, *PARTS[part])
 
-    pltpu.make_async_copy(far, far, l2_recv).wait()
-    whole = tile[1]
-    for dz in range(1, n_z):
-        whole = whole + far[dz - 1]
+    finish_part(part_top, TOP, 1)
+
+    @pl.when(lent)
+    def _():
+        all_of(back.at[0], p2_recv.at[part_first])
+
+    @pl.when(own_first)
+    def _():
+        all_of(back.at[0, pl.ds(0, 7)], p2_recv.at[part_first])
+
+    finish(0, 0)
+
+    @pl.when(jnp.logical_not(leader))
+    def _():
+        all_of(summed, t_recv)
+
+    whole = summed[...]
     lane128 = lax.broadcasted_iota(jnp.int32, (8, 128), 1)
     for e in range(2):
         one = jnp.sum(jnp.where(lane128 == slab * 2 + e, whole, 0.0), axis=1, keepdims=True)
         owned[0, :, e:e + 1] = one[:2]
 
-    finish_part(part_top, TOP, 1)
-
-    @pl.when(lent)
-    def _():
-        all_of(back.at[0], p2_recv.at[part_first])
-
-    @pl.when(own_first)
-    def _():
-        all_of(back.at[0, pl.ds(0, 7)], p2_recv.at[part_first])
-
-    finish(0, 0)
-
     all_of(got.at[pl.ds(1, CV - 1)], p1_send)
     all_of(ret.at[pl.ds(1, CV - 1)], p2_send)
 
@@ -487,7 +502,11 @@
         all_of(w_got.at[pl.ds(3, 4)], w_send.at[1])
 
     pltpu.make_async_copy(near, near, l1_send).wait()
-    pltpu.make_async_copy(far, far, l2_send).wait()
+
+    @pl.when(leader)
+    def _():
+        all_of(far, l2_send)
+        all_of(near, t_send)
 
 
 def hand_over(res, owned, res_out, owned_out, sem):
@@ -521,9 +540,10 @@
             pltpu.VMEM((NY, NX), F32),
             pltpu.VMEM((2, 2, NY, NX), F32),
             pltpu.VMEM((2, 8, 128), F32), pltpu.VMEM((3, 8, 128), F32), pltpu.VMEM((N_SLAB // 4 - 1, 8, 128), F32),
+            pltpu.VMEM((8, 128), F32),
             dma((6,)), dma, dma((len(PARTS) + 2,)), dma, dma((len(PARTS) + 2,)), dma, dma((2,)), dma((2,)), dma, dma, dma, dma, dma,
             dma((2,)), dma((2,)),
-            dma, dma, dma, dma, pltpu.SemaphoreType.REGULAR((2,)),
+            dma, dma, dma, dma, dma, dma, pltpu.SemaphoreType.REGULAR((2,)),
         ],
         compiler_params=pltpu.CompilerParams(
             collective_id=0, has_side_effects=True, vmem_limit_bytes=52 << 20

time: 37 us -> 36.6 us (0.989); the launches traced: 36.3 us -> 36.4 us
  no operation moved by 1% of the time
where the time goes in v7:
time: 36.6 us; the launch traced here: 36.4 us
  Pallas kernels  35.7 us (98%)
  between operations  0.64 us (2%)
    pallas_call x1, Pallas kernels, on_device(): pl.pallas_call(kernel, out_shape=(jax.ShapeDtypeStruct((1,) + block, F32)...  34.7 us
    pallas_call x1, Pallas kernels, on_device(): pl.pallas_call(hand_over, out_shape=tuple((jax.ShapeDtypeStruct(m.shape,...  0.99 us

profile of v7, /device:TPU:1, one launch (start us, length us, event | category | flops | bytes accessed | tf_op | source)
XLA Modules:
  0.0 36.4 jit_solution(14455699371198615853)
XLA Ops:
  0.6 34.7 %shard_map.77 = (f32[1,8,64,512]{3,2,1,0:T(8,128)S(1)}, f32[1,2,2]{2,1,0:T(2,128)S(1)}) custom-call(f32[1,8,64,512]{3,2,1,0:T(8,128)} %vf.1, f32[1,8,64,512]{3,2,1,0:T(8,128)} %vu.1, f32[1,8,64,512]{3,2,1,0:T(8,128)} %vv.1, f32[1,8,64,512]{3,2,1,0:T(8,128)} %vw.1, s32[1,8,64,512]{3,2,1,0:T(8,128)} %wet.1, s32[8,64,512]{2,1,0:T(8,128)} %sec.1), custom_call_target="tpu_custom_call" | custom-call | flops 20000000 | bytes 8388608 | tf_op jit(solution)/shard_map/pallas_call | solution.py:526
  35.4 1.0 %shard_map.78 = (f32[1,8,64,512]{3,2,1,0:T(8,128)}, f32[1,2,2]{2,1,0:T(2,128)}) custom-call(f32[1,8,64,512]{3,2,1,0:T(8,128)S(1)} %get-tuple-element.4.res, f32[1,2,2]{2,1,0:T(2,128)S(1)} %get-tuple-element.5.owned), custom_call_target="tpu_custom_call" | custom-call | tf_op jit(solution)/shard_map/pallas_call | solution.py:553

commit v8 on v7

--- a/solution.py
+++ b/solution.py
@@ -102,11 +102,12 @@
     def strip(n):
         return pl.ds(pl.multiple_of(n * STRIP, STRIP), STRIP)
 
-    def send_out(part, first, count):
+    def send_out(part, first, count, peers=PEERS):
         layers = pl.ds(first, count)
-        for k, (dx, dy) in enumerate(PEERS):
+        for dx, dy in peers:
             peer = to(dx, dy)
-            remote(vf.at[0, layers, strip(peer)], got.at[layers, k], p1_send, p1_recv.at[part], (peer, slab)).start()
+            src = vf.at[0, layers, strip(peer)] if part in (0, part_top) else a_s.at[layers, strip(peer)]
+            remote(src, got.at[layers, slot[(dx, dy)]], p1_send, p1_recv.at[part], (peer, slab)).start()
 
     n_parts = len(PARTS)
     part_top, part_first = n_parts, n_parts + 1
@@ -137,8 +138,9 @@
     def _():
         lend(same_half)
 
-    send_out(0, *PARTS[0])
-    send_out(part_top, TOP, 1)
+    for peers in (PEERS[:4], PEERS[4:]):
+        send_out(0, *PARTS[0], peers)
+        send_out(part_top, TOP, 1, peers)
 
     def send_w(pairs, n):
         for k, (dx, dy) in enumerate(pairs):

time: 36.6 us -> 36.6 us (level)
  no operation moved by 1% of the time
where the time goes in v8:
time: 36.6 us; the launch traced here: 36.4 us
  Pallas kernels  35.7 us (98%)
  between operations  0.64 us (2%)
    pallas_call x1, Pallas kernels, on_device(): pl.pallas_call(kernel, out_shape=(jax.ShapeDtypeStruct((1,) + block, F32)...  34.7 us
    pallas_call x1, Pallas kernels, on_device(): pl.pallas_call(hand_over, out_shape=tuple((jax.ShapeDtypeStruct(m.shape,...  0.99 us

profile of v8, /device:TPU:1, one launch (start us, length us, event | category | flops | bytes accessed | tf_op | source)
XLA Modules:
  0.0 36.4 jit_solution(2970038490385104811)
XLA Ops:
  0.6 34.7 %shard_map.77 = (f32[1,8,64,512]{3,2,1,0:T(8,128)S(1)}, f32[1,2,2]{2,1,0:T(2,128)S(1)}) custom-call(f32[1,8,64,512]{3,2,1,0:T(8,128)} %vf.1, f32[1,8,64,512]{3,2,1,0:T(8,128)} %vu.1, f32[1,8,64,512]{3,2,1,0:T(8,128)} %vv.1, f32[1,8,64,512]{3,2,1,0:T(8,128)} %vw.1, s32[1,8,64,512]{3,2,1,0:T(8,128)} %wet.1, s32[8,64,512]{2,1,0:T(8,128)} %sec.1), custom_call_target="tpu_custom_call" | custom-call | flops 20000000 | bytes 8388608 | tf_op jit(solution)/shard_map/pallas_call | solution.py:528
  35.4 1.0 %shard_map.78 = (f32[1,8,64,512]{3,2,1,0:T(8,128)}, f32[1,2,2]{2,1,0:T(2,128)}) custom-call(f32[1,8,64,512]{3,2,1,0:T(8,128)S(1)} %get-tuple-element.4.res, f32[1,2,2]{2,1,0:T(2,128)S(1)} %get-tuple-element.5.owned), custom_call_target="tpu_custom_call" | custom-call | tf_op jit(solution)/shard_map/pallas_call | solution.py:555
